TPU v7x, 256 devices: a whole 4x4x8 slice. The times are simulated.
256 devices in a mesh: tile: 64 (over y, z, core), view: 4 (over x).
Axes of the slice: x: 4, y: 4, z: 8, core: 2. Of those that a mesh axis runs over, the one named last changes fastest.
Arguments:
- volumes: float32 [64, 4, 4, 512, 512], P('tile', 'view'), may hold values from -6 to 6
- initial_affine: float32 [64, 12], P('tile'), may hold values from -0.5 to 0.5
- slab_start: int32 [64], P('tile'), may hold values from 0 to 448
- margin_rows: int32 [64], P('tile'), may hold values from 16 to 64, as said below
- view_gain: float32 [64, 4], P('tile', 'view'), may hold values from 0.5 to 4
Outputs:
- joined: float32 [64, 4, 512, 512], P('tile', 'view')
- refined: float32 [64, 12], P('tile')
Inputs may be any that keep to these rules, and one draw needn't show every extreme that they name: `margin_rows`: some tile has exactly 64 rows.
All inputs are finite; a program needn't handle non-finite values.
Results may differ from a plain program's by a relative error of at most 0.0003.
Values sent between devices are 32-bit elements; how exact they have to be, the bound alone decides.
A program may use at most 64 MiB of HBM per device.

v0:
```python
import jax
import jax.numpy as jnp
from jax import lax
from jax.sharding import PartitionSpec as P

SLAB = 64
ROUNDS = 2


stiffness_factor = 0.25


def passed_along(block, axis, distance):
    devices = range(lax.axis_size(axis))
    route = [(i - distance, i) for i in devices if i - distance in devices]
    return lax.ppermute(block, axis, route)


def coordinate(count):
    return (jnp.arange(count, dtype=jnp.float32) + 0.5) / count * 2.0 - 1.0


def axis_gradient(array, axis):
    length = array.shape[axis]
    upper = lax.slice_in_dim(array, 2, length, axis=axis)
    lower = lax.slice_in_dim(array, 0, length - 2, axis=axis)
    inner = (upper - lower) * 0.5
    first = lax.slice_in_dim(array, 1, 2, axis=axis) - lax.slice_in_dim(array, 0, 1, axis=axis)
    last = lax.slice_in_dim(array, length - 1, length, axis=axis) - lax.slice_in_dim(
        array, length - 2, length - 1, axis=axis
    )
    return jnp.concatenate([first, inner, last], axis=axis)


def all_gradients(array):
    rank = array.ndim
    return [
        axis_gradient(array, rank - 3),
        axis_gradient(array, rank - 2),
        axis_gradient(array, rank - 1),
    ]


def cholesky_solve(factor, right_side):
    middle = []
    for row in range(12):
        value = right_side[..., row]
        for col in range(row):
            value = value - factor[..., row, col] * middle[col]
        middle.append(value / factor[..., row, row])
    result = [None] * 12
    for row in range(11, -1, -1):
        value = middle[row]
        for col in range(row + 1, 12):
            value = value - factor[..., col, row] * result[col]
        result[row] = value / factor[..., row, row]
    return jnp.stack(result, axis=-1)


def normal_terms(near_slab, window, row_mask, row_coord):
    gradients = all_gradients(window)
    depth = coordinate(window.shape[-3])[:, None, None]
    across = coordinate(window.shape[-1])[None, None, :]
    rows = row_coord[None, :, None]
    basis_terms = [depth, rows, across, 1.0]
    jacobian = jnp.stack(
        [grad_part * basis_part * row_mask for grad_part in gradients for basis_part in basis_terms]
    )
    residual = (near_slab - window) * row_mask
    hessian = jnp.einsum("a...,b...->ab", jacobian, jacobian, precision=lax.Precision.HIGHEST)
    moment = jnp.einsum("a...,...->a", jacobian, residual, precision=lax.Precision.HIGHEST)
    return (hessian, moment)


def correct_volume(volume, affine):
    gradients = all_gradients(volume)
    depth = coordinate(volume.shape[-3])[:, None, None]
    rows = coordinate(volume.shape[-2])[None, :, None]
    across = coordinate(volume.shape[-1])[None, None, :]
    matrix = affine.reshape(3, 4)
    corrected = volume
    for axis_index in range(3):
        shift_field = (
            matrix[axis_index, 0] * depth
            + matrix[axis_index, 1] * rows
            + matrix[axis_index, 2] * across
            + matrix[axis_index, 3]
        )
        corrected = corrected + gradients[axis_index] * shift_field
    return corrected


def matvec(matrix, vector):
    return jnp.dot(matrix, vector, precision=lax.Precision.HIGHEST)


def on_device(volumes, initial_affine, slab_start, margin_rows, view_gain):
    volume = volumes[0, 0]
    depth_count, row_count, across_count = volume.shape
    row_coord = coordinate(row_count)[row_count - SLAB :]
    own_window = lax.dynamic_slice_in_dim(volume, slab_start[0], SLAB, 1)
    window = passed_along(own_window, "tile", -1)
    near_slab = volume[:, row_count - SLAB :, :]
    row_mask = (jnp.arange(SLAB) < margin_rows[0]).astype(jnp.float32)[None, :, None]
    hessian, moment = normal_terms(near_slab, window, row_mask, row_coord)
    hessian, moment = lax.psum((hessian, moment), "view")
    stacked = jnp.concatenate([hessian, moment[:, None]], axis=1)
    lower = passed_along(stacked, "tile", 1)
    hess_low = lower[:, :12]
    moment_low = lower[:, 12]
    view_count = lax.axis_size("view")
    stiffness = stiffness_factor * depth_count * SLAB * across_count * view_count
    factor = jnp.linalg.cholesky(hessian + hess_low + stiffness * jnp.eye(12, dtype=jnp.float32))
    start_params = initial_affine[0]
    params = start_params
    for round_index in range(ROUNDS):
        above = passed_along(params, "tile", -1)
        below = passed_along(params, "tile", 1)
        right_side = (
            matvec(hessian, above)
            - moment
            + matvec(hess_low, below)
            + moment_low
            + stiffness * start_params
        )
        params = cholesky_solve(factor, right_side)
    corrected = correct_volume(volume, params)
    view_index = lax.axis_index("view")
    facing = 1.0 - 2.0 * (view_index % 2).astype(jnp.float32)
    depth = coordinate(depth_count)[:, None, None]
    across = coordinate(across_count)[None, None, :]
    ramp = 0.2 + (1.0 + facing * across) / 2.0
    depth_factor = view_gain[0, 0] * (1.5 + facing * depth)
    weight = depth_factor * ramp
    numerator = (weight * corrected)[None]
    weight_field = jnp.broadcast_to(weight, volume.shape)[None]
    joined_num, joined_den = (
        lax.psum_scatter(numerator, "view", scatter_dimension=1, tiled=True),
        lax.psum_scatter(weight_field, "view", scatter_dimension=1, tiled=True),
    )
    joined = joined_num / joined_den
    return (joined, params[None, :])


def solution(mesh):
    placed = (
        P("tile", "view", None, None, None),
        P("tile", None),
        P("tile"),
        P("tile"),
        P("tile", "view"),
    )
    return jax.shard_map(
        on_device,
        mesh=mesh,
        in_specs=placed,
        out_specs=(P("tile", "view", None, None), P("tile", None)),
        check_vma=False,
    )
```

profile of v0, /device:TPU:24, one launch (start us, length us, event | category | flops | bytes accessed | tf_op | source)
XLA Modules:
  0.0 448.7 jit_solution(15279460595004483955)
XLA Ops:
  7.2 1.9 collective-permute-start.3
  9.1 7.4 %collective-permute-start.1 = (f32[12]{0:T(128)}, f32[12]{0:T(128)S(1)}, u32[]{:S(2)}, u32[]{:S(2)}) collective-permute-start(f32[12]{0:T(128)} %bitcast.262), channel_id=1, source_target_pairs={{4,0},{8,4},{12,8},{16,12},{20,16},{24,20},{28,24},{32,28},{36,32}... | collective-permute-start | bytes 152 | tf_op jit(solution)/shard_map/ppermute | solution.py:16
  17.2 1.1 dynamic-slice_bitcast_fusion
  18.3 2.6 collective-permute-start
  21.0 4.6 %fusion.28 = (f32[1,4,512,1]{3,2,1,0:T(8,128)}, f32[1,4,512,1]{3,2,1,0:T(8,128)}) fusion(f32[4,512,512]{2,1,0:T(8,128)} %bitcast.254), kind=kLoop, calls=%fused_computation.37 | loop fusion | flops 4096 | bytes 49152 | tf_op jit(solution)/shard_map/concatenate | solution.py:32
  25.6 3.1 fusion.5
  28.7 1.8 subtract_bitcast_fusion.1
  31.8 6.5 %fusion.7 = f32[1,4,510,512]{3,2,1,0:T(8,128)} fusion(f32[4,512,512]{2,1,0:T(8,128)} %bitcast.255), kind=kLoop, calls=%fused_computation.9 | loop fusion | flops 2088960 | bytes 12533760 | tf_op jit(solution)/shard_map/concatenate | solution.py:32
  40.9 13.2 %fusion.13 = f32[12,12]{0,1:T(8,128)S(1)} fusion(f32[12,4,64,512]{3,2,1,0:T(8,128)S(1)} %multiply_dynamic-update-slice_fusion), kind=kOutput, calls=%fused_computation.20 | convolution fusion | flops 226492416 | bytes 6292032 | tf_op jit(solution)/shard_map/a...,b...->ab/dot_general | solution.py:70
  54.1 1.2 fusion.30
  55.3 22.5 %fusion.16 = f32[12]{0:T(128)S(1)} fusion(f32[12,4,64,512]{3,2,1,0:T(8,128)S(1)} %multiply_dynamic-update-slice_fusion, f32[4,64,512,1]{2,1,0,3:T(8,128)S(1)} %fusion.30), kind=kOutput, calls=%fused_computation.21 | convolution fusion | flops 18874368 | bytes 6815792 | tf_op jit(solution)/shard_map/a...,...->a/dot_general | solution.py:71
  78.5 10.7 %all-reduce = (f32[12]{0:T(128)S(1)}, f32[12,12]{0,1:T(8,128)S(1)}) all-reduce(f32[12]{0:T(128)S(1)} %fusion.16, f32[12,12]{0,1:T(8,128)S(1)} %fusion.13), channel_id=1, replica_groups=mesh['tile'=64,'view'=4] {'view'}, use_global_device_ids=true, to_apply=%region_1.0 | all-reduce | flops 156 | bytes 1248 | tf_op jit(solution)/shard_map/psum | solution.py:106
  89.2 1.9 collective-permute-start.2
  91.2 5.1 %collective-permute-done.2 = f32[12,13]{0,1:T(8,128)S(1)} collective-permute-done((f32[12,13]{0,1:T(8,128)S(1)}, f32[12,13]{0,1:T(8,128)S(1)}, u32[]{:S(2)}, u32[]{:S(2)}) %collective-permute-start.2) | collective-permute-done | bytes 656 | tf_op jit(solution)/shard_map/ppermute | solution.py:16
  96.4 1.1 cholesky.19
  208.4 1.9 collective-permute-start.5
  210.3 5.8 %collective-permute-start.4 = (f32[12]{0:T(128)S(1)}, f32[12]{0:T(128)S(1)}, u32[]{:S(2)}, u32[]{:S(2)}) collective-permute-start(f32[12]{0:T(128)S(1)} %stack.106), channel_id=1, source_target_pairs={{4,0},{8,4},{12,8},{16,12},{20,16},{24,20},{28,24},{32,28},{36,32}... | collective-permute-start | bytes 152 | tf_op jit(solution)/shard_map/ppermute | solution.py:16
  216.2 1.1 collective-permute-done.4
  327.1 1.2 fusion.49
  328.4 12.4 %fusion.12 = f32[1,4,512,512]{3,2,0,1:T(8,128)} fusion(f32[1,1,512,512]{3,2,1,0:T(8,128)} %get-tuple-element.17, f32[1,2,512,512]{3,2,1,0:T(8,128)S(1)} %multiply_bitcast_fusion, f32[1,1,512,512]{3,2,1,0:T(8,128)} %get-tuple-element.16, f32[1,4,1,512]{3,2,1,0:T(1,128)S(1)} %get-tuple-element.15, f32[1,4,510,512]{3,2,1,0:T(8,128)} %fusion.7, ...), kind=kLoop, calls=%fused_computation.15 | loop fusion | flops 19922944 | bytes 21010444 | tf_op jit(solution)/shard_map/mul | solution.py:135
  340.8 2.5 broadcast_bitcast_fusion
  343.3 43.9 %reduce-scatter.3.cloned.1.call-done = f32[1,1,512,512]{3,2,0,1:T(8,128)} async-done(((f32[1,4,512,512]{3,2,0,1:T(8,128)}), f32[1,1,512,512]{3,2,0,1:T(8,128)}) %reduce-scatter.3.cloned.1.call-update) | async-done | bytes 1048592 | tf_op jit(solution)/shard_map/reduce_scatter | solution.py:138
  387.3 51.8 %reduce-scatter.5.cloned.1.call-done = f32[1,1,512,512]{3,2,0,1:T(8,128)} async-done(((f32[1,4,512,512]{3,2,0,1:T(8,128)}), f32[1,1,512,512]{3,2,0,1:T(8,128)}) %reduce-scatter.5.cloned.1.call-update) | async-done | bytes 1048592 | tf_op jit(solution)/shard_map/reduce_scatter | solution.py:139
  439.1 2.7 divide_bitcast_fusion
  (74 shorter events, 16.0 us)
Async XLA Ops:
  7.2 380.1 %reduce-scatter.3.cloned.1.call-start = ((), (), s32[]{:S(2)}) async-start(), calls=%async_computation.2 | async-start | bytes 5242880 | tf_op jit(solution)/shard_map/reduce_scatter | solution.py:138
  7.2 95.4 %collective-permute-start.3 = (f32[12]{0:T(128)}, f32[12]{0:T(128)S(1)}, u32[]{:S(2)}, u32[]{:S(2)}) collective-permute-start(f32[12]{0:T(128)} %bitcast.261), channel_id=1, source_target_pairs={{0,4},{4,8},{8,12},{12,16},{16,20},{20,24},{24,28},{28,32},{32,36}... | collective-permute-start | bytes 152 | tf_op jit(solution)/shard_map/ppermute | solution.py:16
  9.1 93.6 %collective-permute-start.1 = (f32[12]{0:T(128)}, f32[12]{0:T(128)S(1)}, u32[]{:S(2)}, u32[]{:S(2)}) collective-permute-start(f32[12]{0:T(128)} %bitcast.262), channel_id=1, source_target_pairs={{4,0},{8,4},{12,8},{16,12},{20,16},{24,20},{28,24},{32,28},{36,32}... | collective-permute-start | bytes 152 | tf_op jit(solution)/shard_map/ppermute | solution.py:16
  18.3 20.0 %collective-permute-start = (f32[4,64,512]{2,1,0:T(8,128)S(1)}, f32[4,64,512]{2,1,0:T(8,128)S(1)}, u32[]{:S(2)}, u32[]{:S(2)}) collective-permute-start(f32[4,64,512]{2,1,0:T(8,128)S(1)} %dynamic-slice_bitcast_fusion), channel_id=1, source_target_pairs={{4,0},{8,4},{12,8},{16,12},{20,16},{24,20},{28,24},{32,28},{36,32}... | collective-permute-start | bytes 1572872 | tf_op jit(solution)/shard_map/ppermute | solution.py:16
  21.0 4.6 %copy-start = (f32[1,1,4,512,512]{4,3,2,1,0:T(8,128)S(1)}, f32[1,1,4,512,512]{4,3,2,1,0:T(8,128)}, u32[]{:S(2)}) copy-start(f32[1,1,4,512,512]{4,3,2,1,0:T(8,128)} %param.5) | copy-start | bytes 12582916
  55.3 47.4 %copy-start.3 = (f32[1,12]{1,0:T(1,128)S(1)}, f32[1,12]{1,0:T(1,128)}, u32[]{:S(2)}) copy-start(f32[1,12]{1,0:T(1,128)} %param.6) | copy-start | bytes 148
  55.3 273.1 %copy-start.1 = (f32[1,4,512,1]{3,2,1,0:T(8,128)S(1)}, f32[1,4,512,1]{3,2,1,0:T(8,128)}, u32[]{:S(2)}) copy-start(f32[1,4,512,1]{3,2,1,0:T(8,128)} %get-tuple-element.12) | copy-start | bytes 24580
  89.2 7.1 %collective-permute-start.2 = (f32[12,13]{0,1:T(8,128)S(1)}, f32[12,13]{0,1:T(8,128)S(1)}, u32[]{:S(2)}, u32[]{:S(2)}) collective-permute-start(f32[12,13]{0,1:T(8,128)S(1)} %pad_maximum_fusion.3), channel_id=1, source_target_pairs={{0,4},{4,8},{8,12},{12,16},{16,20},{20,24},{24,28},{28,32},{32,36}... | collective-permute-start | bytes 1880 | tf_op jit(solution)/shard_map/ppermute | solution.py:16
  208.4 7.7 %collective-permute-start.5 = (f32[12]{0:T(128)S(1)}, f32[12]{0:T(128)S(1)}, u32[]{:S(2)}, u32[]{:S(2)}) collective-permute-start(f32[12]{0:T(128)S(1)} %stack.106), channel_id=1, source_target_pairs={{0,4},{4,8},{8,12},{12,16},{16,20},{20,24},{24,28},{28,32},{32,36}... | collective-permute-start | bytes 152 | tf_op jit(solution)/shard_map/ppermute | solution.py:16
  210.3 7.0 %collective-permute-start.4 = (f32[12]{0:T(128)S(1)}, f32[12]{0:T(128)S(1)}, u32[]{:S(2)}, u32[]{:S(2)}) collective-permute-start(f32[12]{0:T(128)S(1)} %stack.106), channel_id=1, source_target_pairs={{4,0},{8,4},{12,8},{16,12},{20,16},{24,20},{28,24},{32,28},{36,32}... | collective-permute-start | bytes 152 | tf_op jit(solution)/shard_map/ppermute | solution.py:16
  321.8 19.0 %copy-start.2 = (f32[12]{0:T(128)}, f32[12]{0:T(128)S(1)}, u32[]{:S(2)}) copy-start(f32[12]{0:T(128)S(1)} %stack.119) | copy-start | bytes 148
  340.8 98.3 %reduce-scatter.5.cloned.1.call-start = ((), (), s32[]{:S(2)}) async-start(), calls=%async_computation.3 | async-start | bytes 5242880 | tf_op jit(solution)/shard_map/reduce_scatter | solution.py:139
Sparse Core Ops, SparseCore 0:
  340.9 46.3 reduce-scatter.2
  390.0 49.0 reduce-scatter.4
where the time goes:
time: 453 us; the launch traced here: 449 us
  between operations  225 us (50%)
  waiting for transfers between devices  102 us (23%)
  other arithmetic  43.7 us (10%)
  matrix products  36.3 us (8%)
  starting transfers between devices  21.6 us (5%)
  blocking collectives  10.7 us (2%)
  local copies, waits for them, and re-layouts  9.78 us (2%)
    reduce_scatter x1, waiting for transfers between devices, on_device(): lax.psum_scatter(weight_field, 'view', scatter_dimension=1, tiled=True)  51.8 us
    reduce_scatter x1, waiting for transfers between devices, on_device(): lax.psum_scatter(numerator, 'view', scatter_dimension=1, tiled=True)  43.9 us
    dot_general x1, matrix products, normal_terms(): jnp.einsum('a...,...->a', jacobian, residual, precision=lax.Precision.HIG...  22.5 us
    ppermute x6, starting transfers between devices, passed_along(): return lax.ppermute(block, axis, route)  21.5 us
    concatenate x12, other arithmetic, axis_gradient(): return jnp.concatenate([first, inner, last], axis=axis)  17.1 us
    dot_general x1, matrix products, normal_terms(): jnp.einsum('a...,b...->ab', jacobian, jacobian, precision=lax.Precision.H...  13.2 us
    mul x1, other arithmetic, on_device(): numerator = (weight * corrected)[None]  12.4 us
    psum x1, blocking collectives, on_device(): hessian, moment = lax.psum((hessian, moment), 'view')  10.7 us
  transfers between devices with their start and end apart: 8, of which 4 were waited for; matrix products, arithmetic and copies ran while one was open for 15% of the time, Pallas kernels for 0%

commit v1 on v0

v1 whole, which is shorter than its diff:
```python
import functools

import jax
import jax.numpy as jnp
from jax import lax
from jax.experimental import pallas as pl
from jax.experimental.pallas import tpu as pltpu
from jax.sharding import PartitionSpec as P

MESH = pl.DeviceIdType.MESH
F32 = jnp.float32
SLAB = 64
HALF_SLAB = 32
SENT_ROWS = 40
STIFFNESS_FACTOR = 0.25
PAD = 8
CHUNK = 64
PAIRS = ((0, 0), (0, 1), (0, 2), (1, 1), (1, 2), (2, 2))
MONOS = ((0, 0), (0, 1), (0, 2), (0, 3), (1, 1), (1, 2), (1, 3), (2, 2), (2, 3), (3, 3))


def iota(shape, dim):
    return lax.broadcasted_iota(jnp.int32, shape, dim)


def coordinate(index, count):
    return (index.astype(F32) + 0.5) * (2.0 / count) - 1.0


def x_gradient(a):
    width = a.shape[-1]
    left = pltpu.roll(a, 1, 1)
    right = pltpu.roll(a, width - 1, 1)
    lane = iota(a.shape, 1)
    inner = (right - left) * 0.5
    return jnp.where(lane == 0, right - a, jnp.where(lane == width - 1, a - left, inner))


def y_gradient(before, a, after):
    top, bottom = iota(a.shape, 0) == 0, iota(a.shape, 0) == 7
    upper = jnp.where(bottom, pltpu.roll(after, 7, 0), pltpu.roll(a, 7, 0))
    lower = jnp.where(top, pltpu.roll(before, 1, 0), pltpu.roll(a, 1, 0))
    return (upper - lower) * 0.5


def z_gradients(p):
    n = len(p)
    inner = [(p[z + 1] - p[z - 1]) * 0.5 for z in range(1, n - 1)]
    return [p[1] - p[0]] + inner + [p[n - 1] - p[n - 2]]


def kernel(
    tiles, views,
    vol, win, aff, margin, gain, out, refined,
    vp, grads, wst, wgrad, wrx, wrx_grad, nrx, mown, mlow, hacc, qacc, cols, buf1, buf2, pcol, xk, snd, rcv, obuf,
    vsem, msem, wsem, nsem, s1, r1, s2, r2, ssem, rsem, osem,
):
    depth, height, width = vol.shape[2:]
    lanes = width // 128
    half = height // 2
    chunks = half // CHUNK
    t = lax.axis_index("tile")
    v = lax.axis_index("view")

    def tile_at(k):
        return lax.rem(t + tiles + k, tiles)

    def view_at(k):
        return lax.rem(v + views + k, views)

    def dev(tile, view):
        return {"tile": tile, "view": view}

    def remote(src, dst, send, recv, device):
        return pltpu.make_async_remote_copy(
            src_ref=src, dst_ref=dst, send_sem=send, recv_sem=recv, device_id=device, device_id_type=MESH
        )

    loads = [pltpu.make_async_copy(vol.at[0, 0, z], vp.at[z, pl.ds(PAD, height)], vsem.at[z]) for z in range(depth)]
    loads.append(pltpu.make_async_copy(win, wst.at[:, pl.ds(PAD, SLAB)], vsem.at[depth]))
    for load in loads:
        load.start()
    barrier = pltpu.get_barrier_semaphore()
    partners = [dev(tile_at(k), v) for k in (-2, -1, 1, 2)] + [dev(t, view_at(k)) for k in range(1, views)]
    for partner in partners:
        pl.semaphore_signal(barrier, inc=1, device_id=partner, device_id_type=MESH)
    mown[...] = jnp.full((8, 128), margin[0], jnp.int32)
    hacc[...] = jnp.zeros_like(hacc)
    qacc[...] = jnp.zeros_like(qacc)
    cols[...] = jnp.zeros_like(cols)
    pl.semaphore_wait(barrier, len(partners))
    send_window = remote(
        win.at[:, pl.ds(0, SENT_ROWS)], wrx.at[:, pl.ds(PAD, SENT_ROWS)], wsem.at[0], wsem.at[1], dev(tile_at(-1), v)
    )
    send_window.start()
    send_margin = remote(mown, mlow, msem.at[0], msem.at[1], dev(tile_at(1), v))
    send_margin.start()
    for load in loads:
        load.wait()
    send_near = remote(
        vp.at[:, pl.ds(PAD + height - HALF_SLAB, HALF_SLAB)], nrx, nsem.at[0], nsem.at[1], dev(tile_at(1), v)
    )
    send_near.start()


    for z in range(depth):
        wst[z, PAD - 1 : PAD, :] = 2.0 * wst[z, PAD : PAD + 1, :] - wst[z, PAD + 1 : PAD + 2, :]
        last = PAD + SLAB - 1
        wst[z, last + 1 : last + 2, :] = 2.0 * wst[z, last : last + 1, :] - wst[z, last - 1 : last, :]
        vp[z, PAD - 1 : PAD, :] = 2.0 * vp[z, PAD : PAD + 1, :] - vp[z, PAD + 1 : PAD + 2, :]
        last = PAD + height - 1
        vp[z, last + 1 : last + 2, :] = 2.0 * vp[z, last : last + 1, :] - vp[z, last - 1 : last, :]

    def gradients_of(src, dst, count):
        def body(r, _):
            r = pl.multiple_of(r * 8, 8)
            planes = [src[z, pl.ds(PAD + r, 8), :] for z in range(depth)]
            for z, g in enumerate(z_gradients(planes)):
                dst[0, z, pl.ds(r, 8), :] = g
            for z in range(depth):
                before, after = src[z, pl.ds(r, 8), :], src[z, pl.ds(2 * PAD + r, 8), :]
                dst[1, z, pl.ds(r, 8), :] = y_gradient(before, planes[z], after)
                dst[2, z, pl.ds(r, 8), :] = x_gradient(planes[z])
            return 0

        lax.fori_loop(0, count // 8, body, 0)

    gradients_of(wst, wgrad, SLAB)

    zc = [(z + 0.5) / depth * 2.0 - 1.0 for z in range(depth)]

    def depth_sum(fields, power):
        return functools.reduce(lambda a, b: a + b, [f * (c**power) if power else f for f, c in zip(fields, zc)])

    sub = iota((8, 128), 0)
    lane8 = iota((8, 128), 1)

    def gradients_at(srcg, r, xs, mask):
        return [[srcg[k, z, pl.ds(r, 8), xs] * mask for z in range(depth)] for k in range(3)]

    def row_coordinate(r):
        return coordinate(sub + (r + height - SLAB), height)

    remote(mown, mlow, msem.at[0], msem.at[1], dev(tile_at(1), v)).wait_recv()
    low_rows = mlow[...]
    own_rows = mown[...]

    def matrix_lanes(xl, _):
        xs = pl.ds(pl.multiple_of(xl * 128, 128), 128)
        xv = coordinate(lane8 + xl * 128, width)

        def body(yb, carry):
            r = pl.multiple_of(yb * 8, 8)
            mask = jnp.where(sub + r < low_rows, 1.0, 0.0).astype(F32)
            g = gradients_at(wgrad, r, xs, mask)
            yv = row_coordinate(r)
            new = []
            for f, (a, b) in enumerate(PAIRS):
                fields = [g[a][z] * g[b][z] for z in range(depth)]
                p0, p1, p2 = (depth_sum(fields, k) for k in range(3))
                yp = yv * p0
                terms = (p2, yv * p1, p1, yv * yp, yp, p0)
                new += [c + term for c, term in zip(carry[6 * f : 6 * f + 6], terms)]
            return tuple(new)

        sums = lax.fori_loop(0, SLAB // 8, body, tuple(jnp.zeros((8, 128), F32) for _ in range(36)))
        for f in range(6):
            zz, zy, zo, yy, yo, oo = sums[6 * f : 6 * f + 6]
            xo = xv * oo
            for m, term in enumerate((zz, zy, xv * zo, zo, yy, xv * yo, yo, xv * xo, xo, oo)):
                hacc[f, m] += term
        return 0

    lax.fori_loop(0, lanes, matrix_lanes, 0)
    for f, (a, b) in enumerate(PAIRS):
        for m, (i, j) in enumerate(MONOS):
            row = jnp.sum(hacc[f, m], axis=0, keepdims=True)
            for p, q in {(4 * a + i, 4 * b + j), (4 * a + j, 4 * b + i), (4 * b + i, 4 * a + j), (4 * b + j, 4 * a + i)}:
                cols[p, q : q + 1, :] = row

    gradients_of(vp, grads, height)

    def moment(part, src, srcg, first, rows, near):
        def lane_block(xl, _):
            xs = pl.ds(pl.multiple_of(xl * 128, 128), 128)
            xv = coordinate(lane8 + xl * 128, width)

            def body(yb, carry):
                r = pl.multiple_of(yb * 8, 8)
                mask = jnp.where(sub + (r + first) < rows, 1.0, 0.0).astype(F32)
                g = gradients_at(srcg, pl.multiple_of(r + first, 8), xs, mask)
                window = [src[z, pl.ds(pl.multiple_of(PAD + first + r, 8), 8), xs] for z in range(depth)]
                residual = [near(z, r, xs) - window[z] for z in range(depth)]
                yv = row_coordinate(r + first)
                new = []
                for k in range(3):
                    fields = [g[k][z] * residual[z] for z in range(depth)]
                    p0, p1 = depth_sum(fields, 0), depth_sum(fields, 1)
                    new += [c + term for c, term in zip(carry[3 * k : 3 * k + 3], (p1, yv * p0, p0))]
                return tuple(new)

            sums = lax.fori_loop(0, HALF_SLAB // 8, body, tuple(jnp.zeros((8, 128), F32) for _ in range(9)))
            for k in range(3):
                zo, yo, oo = sums[3 * k : 3 * k + 3]
                for j, term in enumerate((zo, yo, xv * oo, oo)):
                    qacc[part, 4 * k + j] += term
            return 0

        lax.fori_loop(0, lanes, lane_block, 0)
        for i in range(12):
            cols[12 + part, i : i + 1, :] = jnp.sum(qacc[part, i], axis=0, keepdims=True)

    remote(nrx, nrx, nsem.at[0], nsem.at[1], dev(tile_at(1), v)).wait_recv()
    moment(0, wst, wgrad, HALF_SLAB, low_rows, lambda z, r, xs: nrx[z, pl.ds(r, 8), xs])
    send_window.wait_recv()
    for z in range(depth):
        wrx[z, PAD - 1 : PAD, :] = 2.0 * wrx[z, PAD : PAD + 1, :] - wrx[z, PAD + 1 : PAD + 2, :]
    gradients_of(wrx, wrx_grad, HALF_SLAB)
    moment(1, wrx, wrx_grad, 0, own_rows, lambda z, r, xs: vp[z, pl.ds(PAD + height - SLAB + r, 8), xs])

    row = iota((16, 128), 0)
    lane = iota((16, 128), 1)
    tile_index = row * 0 + t
    has_low = jnp.where(tile_index == 0, 0.0, 1.0).astype(F32)
    has_next = jnp.where(tile_index == tiles - 1, 0.0, 1.0).astype(F32)
    block = jnp.zeros((16, 128), F32)
    for c in range(14):
        total = jnp.sum(cols[c], axis=1, keepdims=True) * (has_next if c == 13 else has_low)
        block = jnp.where(lane == c, total, block)
    buf1[v] = block
    buf1[v, 13:14, :] = jnp.full((1, 128), gain[0, 0], F32)
    shares = [
        remote(buf1.at[v], buf1.at[v], s1.at[k - 1], r1.at[k - 1], dev(t, view_at(k))) for k in range(1, views)
    ]
    for share in shares:
        share.start()
    for k, share in enumerate(shares):
        share.wait_recv()
    total = buf1[0]
    for k in range(1, views):
        total = total + buf1[k]
    buf2[2] = jnp.where(row < 12, total, 0.0)
    buf2[2, 12:13, 0:12] = aff[...]
    passes = [
        remote(buf2.at[2], buf2.at[2 - k], s2.at[i], r2.at[i], dev(tile_at(k), v)) for i, k in enumerate((-2, -1, 1, 2))
    ]
    for passed in passes:
        passed.start()
    for passed in passes:
        passed.wait_recv()

    inside = (row < 12) & (lane < 12)
    blocks = [buf2[k] for k in range(5)]
    below2, below, here, above = [jnp.where(inside, blocks[k + 1], 0.0) for k in range(4)]
    eye = jnp.where((row == lane) & (row < 12), 1.0, 0.0).astype(F32)

    def column(a, k):
        return jnp.broadcast_to(a[:, k : k + 1], (16, 128))

    def lane_sum(a):
        return jnp.broadcast_to(jnp.sum(a, axis=1, keepdims=True), (16, 128))

    def as_row(col):
        return jnp.broadcast_to(jnp.sum(col * eye, axis=0, keepdims=True), (16, 128))

    q = [column(blocks[k + 1], 12) + column(blocks[k], 13) for k in range(4)]
    starts = [jnp.broadcast_to(blocks[k][12:13, :], (16, 128)) for k in range(5)]
    stiff = eye * (STIFFNESS_FACTOR * depth * SLAB * width * views)
    right_up = lane_sum(above * starts[4] + here * starts[2] + stiff * starts[3]) - q[3] + q[2]
    right_down = lane_sum(below * starts[2] + below2 * starts[0] + stiff * starts[1]) - q[1] + q[0]
    right_own = lane_sum(stiff * starts[2]) - q[2] + q[1]
    real = row < 12
    up = jnp.where((lane == 12) & real, right_up, above + here + stiff)
    down = jnp.where((lane == 12) & real, right_down, below + below2 + stiff)
    own = here + below + stiff + pltpu.roll(here, 12, 1) + pltpu.roll(below, 24, 1)
    own = jnp.where((lane == 36) & real, right_own, own)
    systems = [up, down, own]
    for k in range(12):
        for i in range(3):
            a = systems[i]
            col = column(a, k)
            scaled = jnp.broadcast_to(a[k : k + 1, :], (16, 128)) / jnp.broadcast_to(col[k : k + 1, :], (16, 128))
            systems[i] = jnp.where(row == k, scaled, a - col * scaled)
    up, down, own = systems
    first_up, first_down = as_row(column(up, 12)), as_row(column(down, 12))
    mix = pltpu.roll(first_up, 12, 1) + pltpu.roll(first_down, 24, 1) + jnp.where(lane == 36, 1.0, 0.0)
    params = lane_sum(own * mix)
    pcol[...] = params
    refined[...] = as_row(params)[0:1, 0:12]

    def entry(k, j):
        return jnp.broadcast_to(pcol[4 * k + j : 4 * k + j + 1, :], (8, 128))

    facing = 1.0 - 2.0 * lax.rem(v, 2).astype(F32)
    own_gain = gain[0, 0]

    across = coordinate(iota((8, width), 1), width)

    def entry_row(k, j):
        return jnp.concatenate([entry(k, j)] * lanes, axis=1)

    def tables(z, _):
        zf = coordinate(z, depth)
        for k in range(3):
            xk[z, k] = entry_row(k, 0) * zf + entry_row(k, 3) + entry_row(k, 2) * across
        xk[z, 3] = (0.2 + (1.0 + facing * across) * 0.5) * (own_gain * (1.5 + facing * zf))
        return 0

    lax.fori_loop(0, depth, tables, 0)
    slopes = [entry_row(k, 1) for k in range(3)]
    sub_row = iota((8, width), 0)

    def numerator_rows(z, first, dst, dst_first, extra, scale):
        def body(rb, _):
            r = pl.multiple_of(first + rb * 8, 8)
            d = pl.multiple_of(dst_first + rb * 8, 8)
            yv = coordinate(sub_row + r, height)
            value = vp[z, pl.ds(pl.multiple_of(PAD + r, 8), 8), :]
            for k in range(3):
                value = value + grads[k, z, pl.ds(r, 8), :] * (xk[z, k] + slopes[k] * yv)
            value = value * xk[z, 3]
            for stream in extra:
                value = value + rcv[stream, pl.ds(d, 8), :]
            if scale is not None:
                value = value * scale
            dst(d, value)
            return 0

        lax.fori_loop(0, CHUNK // 8, body, 0)

    down_view, up_view, far_view = view_at(-1), view_at(1), view_at(2)

    def hop(stream, c):
        rows = pl.ds(pl.multiple_of(c * CHUNK, CHUNK), CHUNK)
        target = down_view if stream % 2 == 0 else up_view
        return remote(
            snd.at[stream, rows], rcv.at[stream, rows], ssem.at[stream, c], rsem.at[stream, c], dev(t, target)
        )

    def send_chunk(stream, c, plane, upper, extra=()):
        def put(d, value):
            snd[stream, pl.ds(d, 8), :] = value

        c_row = pl.multiple_of(c * CHUNK, CHUNK)
        numerator_rows(plane, (half if upper else 0) + c_row, put, c_row, extra, None)
        hop(stream, c).start()

    def far(c, _):
        send_chunk(0, c, far_view, False)
        send_chunk(1, c, far_view, True)
        return 0

    def near_planes(c, _):
        send_chunk(2, c, down_view, True)
        send_chunk(3, c, up_view, False)
        return 0

    def relay(c, _):
        hop(0, c).wait_recv()
        send_chunk(4, c, down_view, False, (0,))
        hop(1, c).wait_recv()
        send_chunk(5, c, up_view, True, (1,))
        return 0

    lax.fori_loop(0, chunks, far, 0)
    lax.fori_loop(0, chunks, near_planes, 0)
    lax.fori_loop(0, chunks, relay, 0)

    zf = coordinate(v, depth)
    weights = jnp.zeros((8, width), F32)
    for k in range(views):
        s = 1.0 - 2.0 * (k % 2)
        g = jnp.concatenate([jnp.broadcast_to(buf1[k, 13:14, :], (8, 128))] * lanes, axis=1)
        weights = weights + g * (1.5 + s * zf) * (0.2 + (1.0 + s * across) * 0.5)
    inverse = 1.0 / weights

    def write_out(part, c):
        rows = pl.ds(pl.multiple_of(part * half + c * CHUNK, CHUNK), CHUNK)
        return pltpu.make_async_copy(obuf.at[rows], out.at[0, 0, rows], osem.at[part, c])

    def finish(c, _):
        c_row = pl.multiple_of(c * CHUNK, CHUNK)
        for part, streams in ((0, (3, 4)), (1, (2, 5))):
            for stream in streams:
                hop(stream, c).wait_recv()

            def put(d, value, part=part):
                obuf[pl.ds(pl.multiple_of(part * half + d, 8), 8), :] = value

            numerator_rows(v, part * half + c_row, put, c_row, streams, inverse)
            write_out(part, c).start()
        return 0

    lax.fori_loop(0, chunks, finish, 0)

    def drain(c, _):
        for stream in range(6):
            hop(stream, c).wait_send()
        for part in range(2):
            write_out(part, c).wait()
        return 0

    lax.fori_loop(0, chunks, drain, 0)
    send_margin.wait_send()
    send_near.wait_send()
    send_window.wait_send()
    for copy in shares + passes:
        copy.wait_send()


def on_device(tiles, views, volumes, initial_affine, slab_start, margin_rows, view_gain):
    depth, height, width = volumes.shape[2:]
    half = height // 2
    chunks = half // CHUNK
    window = lax.dynamic_slice_in_dim(volumes[0, 0], slab_start[0], SLAB, 1)
    smem = pl.BlockSpec(memory_space=pltpu.SMEM)
    vmem = pl.BlockSpec(memory_space=pltpu.VMEM)
    hbm = pl.BlockSpec(memory_space=pl.ANY)
    dma = pltpu.SemaphoreType.DMA
    return pl.pallas_call(
        functools.partial(kernel, tiles, views),
        out_shape=(jax.ShapeDtypeStruct((1, 1, height, width), F32), jax.ShapeDtypeStruct((1, 12), F32)),
        in_specs=[hbm, hbm, vmem, smem, smem],
        out_specs=(hbm, vmem),
        scratch_shapes=[
            pltpu.VMEM((depth, height + 2 * PAD, width), F32),
            pltpu.VMEM((3, depth, height, width), F32),
            pltpu.VMEM((depth, SLAB + 2 * PAD, width), F32),
            pltpu.VMEM((3, depth, SLAB, width), F32),
            pltpu.VMEM((depth, SENT_ROWS + PAD, width), F32),
            pltpu.VMEM((3, depth, HALF_SLAB, width), F32),
            pltpu.VMEM((depth, HALF_SLAB, width), F32),
            pltpu.VMEM((8, 128), jnp.int32),
            pltpu.VMEM((8, 128), jnp.int32),
            pltpu.VMEM((6, 10, 8, 128), F32),
            pltpu.VMEM((2, 12, 8, 128), F32),
            pltpu.VMEM((14, 16, 128), F32),
            pltpu.VMEM((views, 16, 128), F32),
            pltpu.VMEM((5, 16, 128), F32),
            pltpu.VMEM((16, 128), F32),
            pltpu.VMEM((depth, 4, 8, width), F32),
            pltpu.VMEM((6, half, width), F32),
            pltpu.VMEM((6, half, width), F32),
            pltpu.VMEM((height, width), F32),
            dma((depth + 1,)), dma((2,)), dma((2,)), dma((2,)),
            dma((views - 1,)), dma((views - 1,)), dma((4,)), dma((4,)),
            dma((6, chunks)), dma((6, chunks)), dma((2, chunks)),
        ],
        compiler_params=pltpu.CompilerParams(
            collective_id=0, has_side_effects=True, vmem_limit_bytes=48 * 1024 * 1024
        ),
        name="refine_and_join",
    )(volumes, window, initial_affine, margin_rows, view_gain)


def solution(mesh):
    placed = (
        P("tile", "view", None, None, None),
        P("tile", None),
        P("tile"),
        P("tile"),
        P("tile", "view"),
    )
    return jax.shard_map(
        functools.partial(on_device, mesh.shape["tile"], mesh.shape["view"]),
        mesh=mesh,
        in_specs=placed,
        out_specs=(P("tile", "view", None, None), P("tile", None)),
        check_vma=False,
    )
```

time: 453 us -> 73.9 us (0.16)
  the two profiles are of different devices: /device:TPU:24 before, /device:TPU:1 now
where the time goes in v1:
time: 73.9 us; the launch traced here: 73.7 us
  Pallas kernels  65.7 us (89%)
  local copies, waits for them, and re-layouts  5.46 us (7%)
  between operations  2.6 us (4%)
    pallas_call x1, Pallas kernels, on_device(): pl.pallas_call(functools.partial(kernel, tiles, views), out_shape=(jax.Sh...  65.7 us
    unnamed x6, local copies, waits for them, and re-layouts  4.32 us

profile of v1, /device:TPU:1, one launch (start us, length us, event | category | flops | bytes accessed | tf_op | source)
XLA Modules:
  0.0 73.7 jit_solution(17283519070358592590)
XLA Ops:
  2.6 1.1 %dynamic-slice_bitcast_fusion.win = f32[4,64,512]{2,1,0:T(8,128)S(1)} fusion(f32[1,1,4,512,512]{4,3,2,1,0:T(8,128)} %vol.1, s32[]{:T(128)S(6)} %select_n.3), kind=kLoop, calls=%fused_computation | loop fusion | bytes 1048580 | tf_op jit(solution)/shard_map/dynamic_slice | solution.py:415
  3.7 0.0 copy-start
  3.7 2.2 %copy-done = f32[1,1,4,512,512]{4,3,2,1,0:T(8,128)S(1)} copy-done((f32[1,1,4,512,512]{4,3,2,1,0:T(8,128)S(1)}, f32[1,1,4,512,512]{4,3,2,1,0:T(8,128)}, u32[]{:S(2)}) %copy-start) | copy-done | bytes 4194328
  5.9 0.0 copy-start.1
  5.9 0.7 copy-done.1
  6.6 65.7 %refine_and_join.1 = (f32[1,1,512,512]{3,2,1,0:T(8,128)S(1)}, f32[1,12]{1,0:T(1,128)S(1)}) custom-call(f32[1,1,4,512,512]{4,3,2,1,0:T(8,128)S(1)} %copy-done, f32[4,64,512]{2,1,0:T(8,128)S(1)} %dynamic-slice_bitcast_fusion.win, f32[1,12]{1,0:T(1,128)S(1)} %copy-done.1, s32[1]{0:T(128)S(6)} %copy.10.margin, f32[1,1]{1,0:T(1,128)S(6)} %copy.11.gain), custom_call_target="tpu_custom_call" | custom-call | tf_op jit(solution)/shard_map/refine_and_join/pallas_call | solution.py:420
  72.3 1.0 %copy.12 = f32[1,1,512,512]{3,2,1,0:T(8,128)} copy(f32[1,1,512,512]{3,2,1,0:T(8,128)S(1)} %get-tuple-element.4) | data formatting | bytes 2097152
  73.2 0.5 copy.13
Async XLA Ops:
  3.7 2.2 %copy-start = (f32[1,1,4,512,512]{4,3,2,1,0:T(8,128)S(1)}, f32[1,1,4,512,512]{4,3,2,1,0:T(8,128)}, u32[]{:S(2)}) copy-start(f32[1,1,4,512,512]{4,3,2,1,0:T(8,128)} %vol.1) | copy-start | bytes 12582916
  5.9 0.7 copy-start.1

commit v2 on v1

--- a/solution.py
+++ b/solution.py
@@ -14,7 +14,9 @@
 SENT_ROWS = 40
 STIFFNESS_FACTOR = 0.25
 PAD = 8
-CHUNK = 64
+CHUNK = 32
+RAW_CHUNKS = 5
+EARLY_CHUNKS = 2
 PAIRS = ((0, 0), (0, 1), (0, 2), (1, 1), (1, 2), (2, 2))
 MONOS = ((0, 0), (0, 1), (0, 2), (0, 3), (1, 1), (1, 2), (1, 3), (2, 2), (2, 3), (3, 3))
 
@@ -52,8 +54,8 @@
 def kernel(
     tiles, views,
     vol, win, aff, margin, gain, out, refined,
-    vp, grads, wst, wgrad, wrx, wrx_grad, nrx, mown, mlow, hacc, qacc, cols, buf1, buf2, pcol, xk, snd, rcv, obuf,
-    vsem, msem, wsem, nsem, s1, r1, s2, r2, ssem, rsem, osem,
+    vp, grads, wst, wgrad, wrx, wrx_grad, nrx, mown, mlow, start_affine, hacc, qacc, cols, buf1, buf2, pcol, xk, snd, rcv, obuf, rawv, rawg, wraw,
+    vsem, msem, wsem, nsem, s1, r1, s2, r2, ssem, rsem, osem, rawsem,
 ):
     depth, height, width = vol.shape[2:]
     lanes = width // 128
@@ -68,6 +70,12 @@
     def view_at(k):
         return lax.rem(v + views + k, views)
 
+    def exists(k):
+        return t + k >= 0 if k < 0 else t + k < tiles
+
+    def when_tile(k, action):
+        pl.when(exists(k))(action)
+
     def dev(tile, view):
         return {"tile": tile, "view": view}
 
@@ -78,54 +86,97 @@
 
     loads = [pltpu.make_async_copy(vol.at[0, 0, z], vp.at[z, pl.ds(PAD, height)], vsem.at[z]) for z in range(depth)]
     loads.append(pltpu.make_async_copy(win, wst.at[:, pl.ds(PAD, SLAB)], vsem.at[depth]))
+    loads.append(pltpu.make_async_copy(aff, start_affine, vsem.at[depth + 1]))
     for load in loads:
         load.start()
     barrier = pltpu.get_barrier_semaphore()
-    partners = [dev(tile_at(k), v) for k in (-2, -1, 1, 2)] + [dev(t, view_at(k)) for k in range(1, views)]
-    for partner in partners:
-        pl.semaphore_signal(barrier, inc=1, device_id=partner, device_id_type=MESH)
+    buf2[...] = jnp.zeros_like(buf2)
+    tile_steps = (-2, -1, 1, 2)
+
+    def greet(device):
+        pl.semaphore_signal(barrier, inc=1, device_id=device, device_id_type=MESH)
+
+    for k in tile_steps:
+        when_tile(k, functools.partial(greet, dev(tile_at(k), v)))
+    for k in range(1, views):
+        greet(dev(t, view_at(k)))
     mown[...] = jnp.full((8, 128), margin[0], jnp.int32)
     hacc[...] = jnp.zeros_like(hacc)
     qacc[...] = jnp.zeros_like(qacc)
     cols[...] = jnp.zeros_like(cols)
-    pl.semaphore_wait(barrier, len(partners))
+    peers = views - 1
+    for k in tile_steps:
+        peers = peers + jnp.where(exists(k), 1, 0)
+    pl.semaphore_wait(barrier, peers)
     send_window = remote(
         win.at[:, pl.ds(0, SENT_ROWS)], wrx.at[:, pl.ds(PAD, SENT_ROWS)], wsem.at[0], wsem.at[1], dev(tile_at(-1), v)
     )
-    send_window.start()
+    when_tile(-1, send_window.start)
     send_margin = remote(mown, mlow, msem.at[0], msem.at[1], dev(tile_at(1), v))
-    send_margin.start()
+    when_tile(1, send_margin.start)
     for load in loads:
         load.wait()
     send_near = remote(
         vp.at[:, pl.ds(PAD + height - HALF_SLAB, HALF_SLAB)], nrx, nsem.at[0], nsem.at[1], dev(tile_at(1), v)
     )
-    send_near.start()
-
+    when_tile(1, send_near.start)
+
+    for z in range(depth):
+        vp[z, PAD - 1 : PAD, :] = 2.0 * vp[z, PAD : PAD + 1, :] - vp[z, PAD + 1 : PAD + 2, :]
+        last = PAD + height - 1
+        vp[z, last + 1 : last + 2, :] = 2.0 * vp[z, last : last + 1, :] - vp[z, last - 1 : last, :]
+
+    def depth_gradients_of(src, dst, count):
+        def body(r, _):
+            r = pl.multiple_of(r * 8, 8)
+            planes = [src[z, pl.ds(pl.multiple_of(PAD + r, 8), 8), :] for z in range(depth)]
+            for z, g in enumerate(z_gradients(planes)):
+                dst[0, z, pl.ds(r, 8), :] = g
+            return 0
+
+        lax.fori_loop(0, count // 8, body, 0)
+
+    depth_gradients_of(vp, grads, height)
+
+    down_view, up_view, far_view = view_at(-1), view_at(1), view_at(2)
+    raws = []
+    for part, (first, end) in enumerate(((0, EARLY_CHUNKS * CHUNK), (EARLY_CHUNKS * CHUNK, RAW_CHUNKS * CHUNK))):
+        for side, target in ((0, down_view), (1, up_view)):
+            begin = first + 2 * PAD if part else first
+            size = end + 2 * PAD - begin
+            sems = [rawsem.at[k, 4 * part + side] for k in range(2)]
+            raws.append(
+                remote(
+                    vp.at[far_view, pl.ds(side * half + begin, size)], rawv.at[side, pl.ds(begin, size)], *sems, dev(t, target)
+                )
+            )
+            sems = [rawsem.at[k, 4 * part + 2 + side] for k in range(2)]
+            rows = pl.ds(side * half + first, end - first)
+            raws.append(
+                remote(grads.at[0, far_view, rows], rawg.at[side, pl.ds(first, end - first)], *sems, dev(t, target))
+            )
+    for raw in raws[:4]:
+        raw.start()
 
     for z in range(depth):
         wst[z, PAD - 1 : PAD, :] = 2.0 * wst[z, PAD : PAD + 1, :] - wst[z, PAD + 1 : PAD + 2, :]
         last = PAD + SLAB - 1
         wst[z, last + 1 : last + 2, :] = 2.0 * wst[z, last : last + 1, :] - wst[z, last - 1 : last, :]
-        vp[z, PAD - 1 : PAD, :] = 2.0 * vp[z, PAD : PAD + 1, :] - vp[z, PAD + 1 : PAD + 2, :]
-        last = PAD + height - 1
-        vp[z, last + 1 : last + 2, :] = 2.0 * vp[z, last : last + 1, :] - vp[z, last - 1 : last, :]
-
-    def gradients_of(src, dst, count):
+
+    def gradients_of(src, dst, first, end):
         def body(r, _):
             r = pl.multiple_of(r * 8, 8)
             planes = [src[z, pl.ds(PAD + r, 8), :] for z in range(depth)]
-            for z, g in enumerate(z_gradients(planes)):
-                dst[0, z, pl.ds(r, 8), :] = g
             for z in range(depth):
                 before, after = src[z, pl.ds(r, 8), :], src[z, pl.ds(2 * PAD + r, 8), :]
                 dst[1, z, pl.ds(r, 8), :] = y_gradient(before, planes[z], after)
                 dst[2, z, pl.ds(r, 8), :] = x_gradient(planes[z])
             return 0
 
-        lax.fori_loop(0, count // 8, body, 0)
-
-    gradients_of(wst, wgrad, SLAB)
+        lax.fori_loop(first // 8, end // 8, body, 0)
+
+    depth_gradients_of(wst, wgrad, SLAB)
+    gradients_of(wst, wgrad, 0, SLAB)
 
     zc = [(z + 0.5) / depth * 2.0 - 1.0 for z in range(depth)]
 
@@ -141,7 +192,7 @@
     def row_coordinate(r):
         return coordinate(sub + (r + height - SLAB), height)
 
-    remote(mown, mlow, msem.at[0], msem.at[1], dev(tile_at(1), v)).wait_recv()
+    when_tile(-1, send_margin.wait_recv)
     low_rows = mlow[...]
     own_rows = mown[...]
 
@@ -178,8 +229,6 @@
             for p, q in {(4 * a + i, 4 * b + j), (4 * a + j, 4 * b + i), (4 * b + i, 4 * a + j), (4 * b + j, 4 * a + i)}:
                 cols[p, q : q + 1, :] = row
 
-    gradients_of(vp, grads, height)
-
     def moment(part, src, srcg, first, rows, near):
         def lane_block(xl, _):
             xs = pl.ds(pl.multiple_of(xl * 128, 128), 128)
@@ -210,23 +259,23 @@
         for i in range(12):
             cols[12 + part, i : i + 1, :] = jnp.sum(qacc[part, i], axis=0, keepdims=True)
 
-    remote(nrx, nrx, nsem.at[0], nsem.at[1], dev(tile_at(1), v)).wait_recv()
+    when_tile(-1, send_near.wait_recv)
     moment(0, wst, wgrad, HALF_SLAB, low_rows, lambda z, r, xs: nrx[z, pl.ds(r, 8), xs])
-    send_window.wait_recv()
+    when_tile(1, send_window.wait_recv)
     for z in range(depth):
         wrx[z, PAD - 1 : PAD, :] = 2.0 * wrx[z, PAD : PAD + 1, :] - wrx[z, PAD + 1 : PAD + 2, :]
-    gradients_of(wrx, wrx_grad, HALF_SLAB)
+    depth_gradients_of(wrx, wrx_grad, HALF_SLAB)
+    gradients_of(wrx, wrx_grad, 0, HALF_SLAB)
     moment(1, wrx, wrx_grad, 0, own_rows, lambda z, r, xs: vp[z, pl.ds(PAD + height - SLAB + r, 8), xs])
 
     row = iota((16, 128), 0)
     lane = iota((16, 128), 1)
     tile_index = row * 0 + t
-    has_low = jnp.where(tile_index == 0, 0.0, 1.0).astype(F32)
-    has_next = jnp.where(tile_index == tiles - 1, 0.0, 1.0).astype(F32)
+    has_low, has_next = tile_index > 0, tile_index < tiles - 1
     block = jnp.zeros((16, 128), F32)
     for c in range(14):
-        total = jnp.sum(cols[c], axis=1, keepdims=True) * (has_next if c == 13 else has_low)
-        block = jnp.where(lane == c, total, block)
+        total = jnp.sum(cols[c], axis=1, keepdims=True)
+        block = jnp.where((lane == c) & (has_next if c == 13 else has_low), total, block)
     buf1[v] = block
     buf1[v, 13:14, :] = jnp.full((1, 128), gain[0, 0], F32)
     shares = [
@@ -234,20 +283,24 @@
     ]
     for share in shares:
         share.start()
+    gradients_of(vp, grads, 0, half)
     for k, share in enumerate(shares):
         share.wait_recv()
+    for raw in raws[4:]:
+        raw.start()
     total = buf1[0]
     for k in range(1, views):
         total = total + buf1[k]
     buf2[2] = jnp.where(row < 12, total, 0.0)
-    buf2[2, 12:13, 0:12] = aff[...]
+    buf2[2, 12:13, 0:12] = start_affine[...]
     passes = [
-        remote(buf2.at[2], buf2.at[2 - k], s2.at[i], r2.at[i], dev(tile_at(k), v)) for i, k in enumerate((-2, -1, 1, 2))
+        remote(buf2.at[2], buf2.at[2 - k], s2.at[i], r2.at[i], dev(tile_at(k), v)) for i, k in enumerate(tile_steps)
     ]
-    for passed in passes:
-        passed.start()
-    for passed in passes:
-        passed.wait_recv()
+    for k, passed in zip(tile_steps, passes):
+        when_tile(k, passed.start)
+    gradients_of(vp, grads, half, height)
+    for k, passed in zip(tile_steps, passes):
+        when_tile(-k, passed.wait_recv)
 
     inside = (row < 12) & (lane < 12)
     blocks = [buf2[k] for k in range(5)]
@@ -328,8 +381,6 @@
 
         lax.fori_loop(0, CHUNK // 8, body, 0)
 
-    down_view, up_view, far_view = view_at(-1), view_at(1), view_at(2)
-
     def hop(stream, c):
         rows = pl.ds(pl.multiple_of(c * CHUNK, CHUNK), CHUNK)
         target = down_view if stream % 2 == 0 else up_view
@@ -345,6 +396,32 @@
         numerator_rows(plane, (half if upper else 0) + c_row, put, c_row, extra, None)
         hop(stream, c).start()
 
+    def relay_raw(side, c):
+        plane = (down_view, up_view)[side]
+        stream = 4 + side
+        c_row = pl.multiple_of(c * CHUNK, CHUNK)
+
+        def body(rb, _):
+            d = pl.multiple_of(c_row + rb * 8, 8)
+            r = pl.multiple_of(side * half + d, 8)
+            yv = coordinate(sub_row + r, height)
+            shifts = [xk[plane, k] + slopes[k] * yv for k in range(3)]
+            value = vp[plane, pl.ds(pl.multiple_of(PAD + r, 8), 8), :]
+            for k in range(3):
+                value = value + grads[k, plane, pl.ds(r, 8), :] * shifts[k]
+            before, here_v, after = [rawv[side, pl.ds(pl.multiple_of(d + k * PAD, 8), 8), :] for k in range(3)]
+            other = here_v + rawg[side, pl.ds(d, 8), :] * shifts[0]
+            other = other + y_gradient(before, here_v, after) * shifts[1] + x_gradient(here_v) * shifts[2]
+            snd[stream, pl.ds(d, 8), :] = value * xk[plane, 3] + other * wraw[side]
+            return 0
+
+        lax.fori_loop(0, CHUNK // 8, body, 0)
+        hop(stream, c).start()
+
+    for side, plane, source in ((0, down_view, up_view), (1, up_view, down_view)):
+        g = jnp.concatenate([jnp.broadcast_to(buf1[source, 13:14, :], (8, 128))] * lanes, axis=1)
+        wraw[side] = (0.2 + (1.0 - facing * across) * 0.5) * (g * (1.5 - facing * coordinate(plane, depth)))
+
     def far(c, _):
         send_chunk(0, c, far_view, False)
         send_chunk(1, c, far_view, True)
@@ -362,9 +439,17 @@
         send_chunk(5, c, up_view, True, (1,))
         return 0
 
-    lax.fori_loop(0, chunks, far, 0)
+    def relay_both(c, _):
+        relay_raw(0, c)
+        relay_raw(1, c)
+        return 0
+
+    lax.fori_loop(RAW_CHUNKS, chunks, far, 0)
     lax.fori_loop(0, chunks, near_planes, 0)
-    lax.fori_loop(0, chunks, relay, 0)
+    for raw in raws:
+        raw.wait_recv()
+    lax.fori_loop(0, RAW_CHUNKS, relay_both, 0)
+    lax.fori_loop(RAW_CHUNKS, chunks, relay, 0)
 
     zf = coordinate(v, depth)
     weights = jnp.zeros((8, width), F32)
@@ -394,17 +479,25 @@
     lax.fori_loop(0, chunks, finish, 0)
 
     def drain(c, _):
-        for stream in range(6):
+        for stream in range(2, 6):
             hop(stream, c).wait_send()
         for part in range(2):
             write_out(part, c).wait()
         return 0
 
+    def drain_far(c, _):
+        hop(0, c).wait_send()
+        hop(1, c).wait_send()
+        return 0
+
     lax.fori_loop(0, chunks, drain, 0)
-    send_margin.wait_send()
-    send_near.wait_send()
-    send_window.wait_send()
-    for copy in shares + passes:
+    lax.fori_loop(RAW_CHUNKS, chunks, drain_far, 0)
+    when_tile(1, send_margin.wait_send)
+    when_tile(1, send_near.wait_send)
+    when_tile(-1, send_window.wait_send)
+    for k, passed in zip(tile_steps, passes):
+        when_tile(k, passed.wait_send)
+    for copy in shares + raws:
         copy.wait_send()
 
 
@@ -415,13 +508,13 @@
     window = lax.dynamic_slice_in_dim(volumes[0, 0], slab_start[0], SLAB, 1)
     smem = pl.BlockSpec(memory_space=pltpu.SMEM)
     vmem = pl.BlockSpec(memory_space=pltpu.VMEM)
-    hbm = pl.BlockSpec(memory_space=pl.ANY)
+    anywhere = pl.BlockSpec(memory_space=pl.ANY)
     dma = pltpu.SemaphoreType.DMA
     return pl.pallas_call(
         functools.partial(kernel, tiles, views),
         out_shape=(jax.ShapeDtypeStruct((1, 1, height, width), F32), jax.ShapeDtypeStruct((1, 12), F32)),
-        in_specs=[hbm, hbm, vmem, smem, smem],
-        out_specs=(hbm, vmem),
+        in_specs=[pl.BlockSpec(memory_space=pltpu.HBM), anywhere, pl.BlockSpec(memory_space=pltpu.HBM), smem, smem],
+        out_specs=(anywhere, vmem),
         scratch_shapes=[
             pltpu.VMEM((depth, height + 2 * PAD, width), F32),
             pltpu.VMEM((3, depth, height, width), F32),
@@ -432,6 +525,7 @@
             pltpu.VMEM((depth, HALF_SLAB, width), F32),
             pltpu.VMEM((8, 128), jnp.int32),
             pltpu.VMEM((8, 128), jnp.int32),
+            pltpu.VMEM((1, 12), F32),
             pltpu.VMEM((6, 10, 8, 128), F32),
             pltpu.VMEM((2, 12, 8, 128), F32),
             pltpu.VMEM((14, 16, 128), F32),
@@ -442,15 +536,24 @@
             pltpu.VMEM((6, half, width), F32),
             pltpu.VMEM((6, half, width), F32),
             pltpu.VMEM((height, width), F32),
-            dma((depth + 1,)), dma((2,)), dma((2,)), dma((2,)),
+            pltpu.VMEM((2, RAW_CHUNKS * CHUNK + 2 * PAD, width), F32),
+            pltpu.VMEM((2, RAW_CHUNKS * CHUNK, width), F32),
+            pltpu.VMEM((2, 8, width), F32),
+            dma((depth + 2,)), dma((2,)), dma((2,)), dma((2,)),
             dma((views - 1,)), dma((views - 1,)), dma((4,)), dma((4,)),
-            dma((6, chunks)), dma((6, chunks)), dma((2, chunks)),
+            dma((6, chunks)), dma((6, chunks)), dma((2, chunks)), dma((2, 8)),
         ],
         compiler_params=pltpu.CompilerParams(
-            collective_id=0, has_side_effects=True, vmem_limit_bytes=48 * 1024 * 1024
+            collective_id=0, has_side_effects=True, vmem_limit_bytes=52 * 1024 * 1024
         ),
         name="refine_and_join",
-    )(volumes, window, initial_affine, margin_rows, view_gain)
+    )(
+        pltpu.with_memory_space_constraint(volumes, pltpu.HBM),
+        window,
+        pltpu.with_memory_space_constraint(initial_affine, pltpu.HBM),
+        margin_rows,
+        view_gain,
+    )
 
 
 def solution(mesh):

time: 73.9 us -> 60 us (0.81)
  the two profiles are of different devices: /device:TPU:1 before, /device:TPU:24 now
where the time goes in v2:
time: 60 us; the launch traced here: 59.8 us
  Pallas kernels  54.6 us (91%)
  local copies, waits for them, and re-layouts  2.63 us (4%)
  between operations  2.59 us (4%)
    pallas_call x1, Pallas kernels, on_device(): pl.pallas_call(functools.partial(kernel, tiles, views), out_shape=(jax.Sh...  54.6 us
    unnamed x2, local copies, waits for them, and re-layouts  1.48 us

profile of v2, /device:TPU:24, one launch (start us, length us, event | category | flops | bytes accessed | tf_op | source)
XLA Modules:
  0.0 59.8 jit_solution(6018176633292992151)
XLA Ops:
  2.6 1.1 %dynamic-slice_bitcast_fusion.win = f32[4,64,512]{2,1,0:T(8,128)S(1)} fusion(f32[1,1,4,512,512]{4,3,2,1,0:T(8,128)} %vol.1, s32[]{:T(128)S(6)} %select_n.3), kind=kLoop, calls=%fused_computation | loop fusion | bytes 1048580 | tf_op jit(solution)/shard_map/dynamic_slice | solution.py:508
  3.7 54.6 %refine_and_join.1 = (f32[1,1,512,512]{3,2,1,0:T(8,128)S(1)}, f32[1,12]{1,0:T(1,128)S(1)}) custom-call(f32[1,1,4,512,512]{4,3,2,1,0:T(8,128)} %vol.1, f32[4,64,512]{2,1,0:T(8,128)S(1)} %dynamic-slice_bitcast_fusion.win, f32[1,12]{1,0:T(1,128)} %aff.1, s32[1]{0:T(128)S(6)} %copy.10.margin, f32[1,1]{1,0:T(1,128)S(6)} %copy.11.gain), custom_call_target="tpu_custom_call" | custom-call | tf_op jit(solution)/shard_map/refine_and_join/pallas_call | solution.py:513
  58.4 1.0 %copy.12 = f32[1,1,512,512]{3,2,1,0:T(8,128)} copy(f32[1,1,512,512]{3,2,1,0:T(8,128)S(1)} %get-tuple-element.4) | data formatting | bytes 2097152
  59.3 0.5 copy.13

commit v3 on v2

--- a/solution.py
+++ b/solution.py
@@ -16,7 +16,7 @@
 PAD = 8
 CHUNK = 32
 RAW_CHUNKS = 5
-EARLY_CHUNKS = 2
+EARLY_ROWS = 96
 PAIRS = ((0, 0), (0, 1), (0, 2), (1, 1), (1, 2), (2, 2))
 MONOS = ((0, 0), (0, 1), (0, 2), (0, 3), (1, 1), (1, 2), (1, 3), (2, 2), (2, 3), (3, 3))
 
@@ -53,7 +53,7 @@
 
 def kernel(
     tiles, views,
-    vol, win, aff, margin, gain, out, refined,
+    vol, aff, slab, margin, gain, out, refined,
     vp, grads, wst, wgrad, wrx, wrx_grad, nrx, mown, mlow, start_affine, hacc, qacc, cols, buf1, buf2, pcol, xk, snd, rcv, obuf, rawv, rawg, wraw,
     vsem, msem, wsem, nsem, s1, r1, s2, r2, ssem, rsem, osem, rawsem,
 ):
@@ -85,8 +85,7 @@
         )
 
     loads = [pltpu.make_async_copy(vol.at[0, 0, z], vp.at[z, pl.ds(PAD, height)], vsem.at[z]) for z in range(depth)]
-    loads.append(pltpu.make_async_copy(win, wst.at[:, pl.ds(PAD, SLAB)], vsem.at[depth]))
-    loads.append(pltpu.make_async_copy(aff, start_affine, vsem.at[depth + 1]))
+    loads.append(pltpu.make_async_copy(aff, start_affine, vsem.at[depth]))
     for load in loads:
         load.start()
     barrier = pltpu.get_barrier_semaphore()
@@ -108,19 +107,44 @@
     for k in tile_steps:
         peers = peers + jnp.where(exists(k), 1, 0)
     pl.semaphore_wait(barrier, peers)
+    send_margin = remote(mown, mlow, msem.at[0], msem.at[1], dev(tile_at(1), v))
+    when_tile(1, send_margin.start)
+    send_near = remote(
+        vol.at[0, 0, :, pl.ds(height - HALF_SLAB, HALF_SLAB)], nrx, nsem.at[0], nsem.at[1], dev(tile_at(1), v)
+    )
+    when_tile(1, send_near.start)
+
+    down_view, up_view, far_view = view_at(-1), view_at(1), view_at(2)
+    raws = []
+    for part, (first, end) in enumerate(((0, EARLY_ROWS), (EARLY_ROWS, RAW_CHUNKS * CHUNK))):
+        for side, target in ((0, down_view), (1, up_view)):
+            begin = first + PAD if part else first - side * PAD
+            source = vol.at[0, 0, far_view, pl.ds(side * half + begin, end + PAD - begin)]
+            landing = rawv.at[side, pl.ds(PAD + begin, end + PAD - begin)]
+            raws.append(remote(source, landing, rawsem.at[0, 4 * part + side], rawsem.at[1, 4 * part + side], dev(t, target)))
+        for side, target in ((0, down_view), (1, up_view)):
+            sems = [rawsem.at[k, 4 * part + 2 + side] for k in range(2)]
+            rows = pl.ds(side * half + first, end - first)
+            raws.append(
+                remote(grads.at[0, far_view, rows], rawg.at[side, pl.ds(first, end - first)], *sems, dev(t, target))
+            )
+    for raw in raws[:2]:
+        raw.start()
+    for load in loads:
+        load.wait()
+    start = slab[0]
+    aligned = lax.div(start, 8) * 8
+    shift = jnp.full((SLAB + 8, width), start - aligned, jnp.int32)
+    moves = [(k, lax.bitwise_and(shift, k) != 0) for k in (1, 2, 4)]
+    for z in range(depth):
+        rows = vp[z, pl.ds(aligned + PAD, SLAB + 8), :]
+        for k, moved in moves:
+            rows = jnp.where(moved, pltpu.roll(rows, SLAB + 8 - k, 0), rows)
+        wst[z, PAD : PAD + SLAB, :] = rows[:SLAB]
     send_window = remote(
-        win.at[:, pl.ds(0, SENT_ROWS)], wrx.at[:, pl.ds(PAD, SENT_ROWS)], wsem.at[0], wsem.at[1], dev(tile_at(-1), v)
+        wst.at[:, pl.ds(PAD, SENT_ROWS)], wrx.at[:, pl.ds(PAD, SENT_ROWS)], wsem.at[0], wsem.at[1], dev(tile_at(-1), v)
     )
     when_tile(-1, send_window.start)
-    send_margin = remote(mown, mlow, msem.at[0], msem.at[1], dev(tile_at(1), v))
-    when_tile(1, send_margin.start)
-    for load in loads:
-        load.wait()
-    send_near = remote(
-        vp.at[:, pl.ds(PAD + height - HALF_SLAB, HALF_SLAB)], nrx, nsem.at[0], nsem.at[1], dev(tile_at(1), v)
-    )
-    when_tile(1, send_near.start)
-
     for z in range(depth):
         vp[z, PAD - 1 : PAD, :] = 2.0 * vp[z, PAD : PAD + 1, :] - vp[z, PAD + 1 : PAD + 2, :]
         last = PAD + height - 1
@@ -138,24 +162,7 @@
 
     depth_gradients_of(vp, grads, height)
 
-    down_view, up_view, far_view = view_at(-1), view_at(1), view_at(2)
-    raws = []
-    for part, (first, end) in enumerate(((0, EARLY_CHUNKS * CHUNK), (EARLY_CHUNKS * CHUNK, RAW_CHUNKS * CHUNK))):
-        for side, target in ((0, down_view), (1, up_view)):
-            begin = first + 2 * PAD if part else first
-            size = end + 2 * PAD - begin
-            sems = [rawsem.at[k, 4 * part + side] for k in range(2)]
-            raws.append(
-                remote(
-                    vp.at[far_view, pl.ds(side * half + begin, size)], rawv.at[side, pl.ds(begin, size)], *sems, dev(t, target)
-                )
-            )
-            sems = [rawsem.at[k, 4 * part + 2 + side] for k in range(2)]
-            rows = pl.ds(side * half + first, end - first)
-            raws.append(
-                remote(grads.at[0, far_view, rows], rawg.at[side, pl.ds(first, end - first)], *sems, dev(t, target))
-            )
-    for raw in raws[:4]:
+    for raw in raws[2:4]:
         raw.start()
 
     for z in range(depth):
@@ -286,8 +293,6 @@
     gradients_of(vp, grads, 0, half)
     for k, share in enumerate(shares):
         share.wait_recv()
-    for raw in raws[4:]:
-        raw.start()
     total = buf1[0]
     for k in range(1, views):
         total = total + buf1[k]
@@ -298,7 +303,29 @@
     ]
     for k, passed in zip(tile_steps, passes):
         when_tile(k, passed.start)
+    for raw in raws[4:]:
+        raw.start()
     gradients_of(vp, grads, half, height)
+    across = coordinate(iota((8, width), 1), width)
+    facing = 1.0 - 2.0 * lax.rem(v, 2).astype(F32)
+
+    def plane_weights(z, _):
+        xk[z, 3] = (0.2 + (1.0 + facing * across) * 0.5) * (gain[0, 0] * (1.5 + facing * coordinate(z, depth)))
+        return 0
+
+    lax.fori_loop(0, depth, plane_weights, 0)
+    for side, plane, source in ((0, down_view, up_view), (1, up_view, down_view)):
+        g = jnp.concatenate([jnp.broadcast_to(buf1[source, 13:14, :], (8, 128))] * lanes, axis=1)
+        wraw[side] = (0.2 + (1.0 - facing * across) * 0.5) * (g * (1.5 - facing * coordinate(plane, depth)))
+
+    zf = coordinate(v, depth)
+    weights = jnp.zeros((8, width), F32)
+    for k in range(views):
+        s = 1.0 - 2.0 * (k % 2)
+        g = jnp.concatenate([jnp.broadcast_to(buf1[k, 13:14, :], (8, 128))] * lanes, axis=1)
+        weights = weights + g * (1.5 + s * zf) * (0.2 + (1.0 + s * across) * 0.5)
+    inverse = 1.0 / weights
+
     for k, passed in zip(tile_steps, passes):
         when_tile(-k, passed.wait_recv)
 
@@ -332,7 +359,7 @@
         for i in range(3):
             a = systems[i]
             col = column(a, k)
-            scaled = jnp.broadcast_to(a[k : k + 1, :], (16, 128)) / jnp.broadcast_to(col[k : k + 1, :], (16, 128))
+            scaled = jnp.broadcast_to(a[k : k + 1, :] / col[k : k + 1, :], (16, 128))
             systems[i] = jnp.where(row == k, scaled, a - col * scaled)
     up, down, own = systems
     first_up, first_down = as_row(column(up, 12)), as_row(column(down, 12))
@@ -344,11 +371,6 @@
     def entry(k, j):
         return jnp.broadcast_to(pcol[4 * k + j : 4 * k + j + 1, :], (8, 128))
 
-    facing = 1.0 - 2.0 * lax.rem(v, 2).astype(F32)
-    own_gain = gain[0, 0]
-
-    across = coordinate(iota((8, width), 1), width)
-
     def entry_row(k, j):
         return jnp.concatenate([entry(k, j)] * lanes, axis=1)
 
@@ -356,7 +378,6 @@
         zf = coordinate(z, depth)
         for k in range(3):
             xk[z, k] = entry_row(k, 0) * zf + entry_row(k, 3) + entry_row(k, 2) * across
-        xk[z, 3] = (0.2 + (1.0 + facing * across) * 0.5) * (own_gain * (1.5 + facing * zf))
         return 0
 
     lax.fori_loop(0, depth, tables, 0)
@@ -418,10 +439,6 @@
         lax.fori_loop(0, CHUNK // 8, body, 0)
         hop(stream, c).start()
 
-    for side, plane, source in ((0, down_view, up_view), (1, up_view, down_view)):
-        g = jnp.concatenate([jnp.broadcast_to(buf1[source, 13:14, :], (8, 128))] * lanes, axis=1)
-        wraw[side] = (0.2 + (1.0 - facing * across) * 0.5) * (g * (1.5 - facing * coordinate(plane, depth)))
-
     def far(c, _):
         send_chunk(0, c, far_view, False)
         send_chunk(1, c, far_view, True)
@@ -448,16 +465,9 @@
     lax.fori_loop(0, chunks, near_planes, 0)
     for raw in raws:
         raw.wait_recv()
+    rawv[0, PAD - 1 : PAD, :] = 2.0 * rawv[0, PAD : PAD + 1, :] - rawv[0, PAD + 1 : PAD + 2, :]
     lax.fori_loop(0, RAW_CHUNKS, relay_both, 0)
     lax.fori_loop(RAW_CHUNKS, chunks, relay, 0)
-
-    zf = coordinate(v, depth)
-    weights = jnp.zeros((8, width), F32)
-    for k in range(views):
-        s = 1.0 - 2.0 * (k % 2)
-        g = jnp.concatenate([jnp.broadcast_to(buf1[k, 13:14, :], (8, 128))] * lanes, axis=1)
-        weights = weights + g * (1.5 + s * zf) * (0.2 + (1.0 + s * across) * 0.5)
-    inverse = 1.0 / weights
 
     def write_out(part, c):
         rows = pl.ds(pl.multiple_of(part * half + c * CHUNK, CHUNK), CHUNK)
@@ -505,7 +515,6 @@
     depth, height, width = volumes.shape[2:]
     half = height // 2
     chunks = half // CHUNK
-    window = lax.dynamic_slice_in_dim(volumes[0, 0], slab_start[0], SLAB, 1)
     smem = pl.BlockSpec(memory_space=pltpu.SMEM)
     vmem = pl.BlockSpec(memory_space=pltpu.VMEM)
     anywhere = pl.BlockSpec(memory_space=pl.ANY)
@@ -513,7 +522,7 @@
     return pl.pallas_call(
         functools.partial(kernel, tiles, views),
         out_shape=(jax.ShapeDtypeStruct((1, 1, height, width), F32), jax.ShapeDtypeStruct((1, 12), F32)),
-        in_specs=[pl.BlockSpec(memory_space=pltpu.HBM), anywhere, pl.BlockSpec(memory_space=pltpu.HBM), smem, smem],
+        in_specs=[pl.BlockSpec(memory_space=pltpu.HBM), pl.BlockSpec(memory_space=pltpu.HBM), smem, smem, smem],
         out_specs=(anywhere, vmem),
         scratch_shapes=[
             pltpu.VMEM((depth, height + 2 * PAD, width), F32),
@@ -539,7 +548,7 @@
             pltpu.VMEM((2, RAW_CHUNKS * CHUNK + 2 * PAD, width), F32),
             pltpu.VMEM((2, RAW_CHUNKS * CHUNK, width), F32),
             pltpu.VMEM((2, 8, width), F32),
-            dma((depth + 2,)), dma((2,)), dma((2,)), dma((2,)),
+            dma((depth + 1,)), dma((2,)), dma((2,)), dma((2,)),
             dma((views - 1,)), dma((views - 1,)), dma((4,)), dma((4,)),
             dma((6, chunks)), dma((6, chunks)), dma((2, chunks)), dma((2, 8)),
         ],
@@ -549,8 +558,8 @@
         name="refine_and_join",
     )(
         pltpu.with_memory_space_constraint(volumes, pltpu.HBM),
-        window,
         pltpu.with_memory_space_constraint(initial_affine, pltpu.HBM),
+        slab_start,
         margin_rows,
         view_gain,
     )

time: 60 us -> 58.5 us (0.975)
  local copies, waits for them, and re-layouts: 2.63 us -> 1.48 us
    dynamic_slice x1 -> x0, local copies, waits for them, and re-layouts: 1.14 us -> none  [on_device(): window = lax.dynamic_slice_in_dim(volumes[0, 0], slab_start[0], SLAB, 1)]
where the time goes in v3:
time: 58.5 us; the launch traced here: 58.4 us
  Pallas kernels  54.3 us (93%)
  between operations  2.58 us (4%)
  local copies, waits for them, and re-layouts  1.48 us (3%)
    pallas_call x1, Pallas kernels, on_device(): pl.pallas_call(functools.partial(kernel, tiles, views), out_shape=(jax.Sh...  54.3 us
    unnamed x2, local copies, waits for them, and re-layouts  1.48 us

profile of v3, /device:TPU:24, one launch (start us, length us, event | category | flops | bytes accessed | tf_op | source)
XLA Modules:
  0.0 58.4 jit_solution(6436357437065982789)
XLA Ops:
  2.6 54.3 %refine_and_join.1 = (f32[1,1,512,512]{3,2,1,0:T(8,128)S(1)}, f32[1,12]{1,0:T(1,128)S(1)}) custom-call(f32[1,1,4,512,512]{4,3,2,1,0:T(8,128)} %vol.1, f32[1,12]{1,0:T(1,128)} %aff.1, s32[1]{0:T(128)S(6)} %copy.9.slab, s32[1]{0:T(128)S(6)} %copy.10.margin, f32[1,1]{1,0:T(1,128)S(6)} %copy.11.gain), custom_call_target="tpu_custom_call" | custom-call | tf_op jit(solution)/shard_map/refine_and_join/pallas_call | solution.py:522
  56.9 1.0 %copy.12 = f32[1,1,512,512]{3,2,1,0:T(8,128)} copy(f32[1,1,512,512]{3,2,1,0:T(8,128)S(1)} %get-tuple-element.4) | data formatting | bytes 2097152
  57.9 0.5 copy.13

commit v4 on v3

--- a/solution.py
+++ b/solution.py
@@ -54,8 +54,8 @@
 def kernel(
     tiles, views,
     vol, aff, slab, margin, gain, out, refined,
-    vp, grads, wst, wgrad, wrx, wrx_grad, nrx, mown, mlow, start_affine, hacc, qacc, cols, buf1, buf2, pcol, xk, snd, rcv, obuf, rawv, rawg, wraw,
-    vsem, msem, wsem, nsem, s1, r1, s2, r2, ssem, rsem, osem, rawsem,
+    vp, grads, wst, wgrad, wrx, wrx_grad, nrx, mown, mlow, start_affine, hacc, qacc, cols, buf1, buf2, pcol, xk, snd, rcv, rawv, rawg, wraw,
+    vsem, msem, wsem, nsem, s1, r1, s2, r2, ssem, rsem, rawsem,
 ):
     depth, height, width = vol.shape[2:]
     lanes = width // 128
@@ -130,21 +130,23 @@
             )
     for raw in raws[:2]:
         raw.start()
-    for load in loads:
-        load.wait()
     start = slab[0]
     aligned = lax.div(start, 8) * 8
     shift = jnp.full((SLAB + 8, width), start - aligned, jnp.int32)
     moves = [(k, lax.bitwise_and(shift, k) != 0) for k in (1, 2, 4)]
+    for load in loads:
+        load.wait()
+    send_windows = []
     for z in range(depth):
         rows = vp[z, pl.ds(aligned + PAD, SLAB + 8), :]
         for k, moved in moves:
             rows = jnp.where(moved, pltpu.roll(rows, SLAB + 8 - k, 0), rows)
         wst[z, PAD : PAD + SLAB, :] = rows[:SLAB]
-    send_window = remote(
-        wst.at[:, pl.ds(PAD, SENT_ROWS)], wrx.at[:, pl.ds(PAD, SENT_ROWS)], wsem.at[0], wsem.at[1], dev(tile_at(-1), v)
-    )
-    when_tile(-1, send_window.start)
+        sent = pl.ds(PAD, SENT_ROWS)
+        send_windows.append(
+            remote(wst.at[z, sent], wrx.at[z, sent], wsem.at[0, z], wsem.at[1, z], dev(tile_at(-1), v))
+        )
+        when_tile(-1, send_windows[z].start)
     for z in range(depth):
         vp[z, PAD - 1 : PAD, :] = 2.0 * vp[z, PAD : PAD + 1, :] - vp[z, PAD + 1 : PAD + 2, :]
         last = PAD + height - 1
@@ -266,23 +268,30 @@
         for i in range(12):
             cols[12 + part, i : i + 1, :] = jnp.sum(qacc[part, i], axis=0, keepdims=True)
 
+    row = iota((16, 128), 0)
+    lane = iota((16, 128), 1)
+    tile_index = row * 0 + t
+    has_low, has_next = tile_index > 0, tile_index < tiles - 1
+    block = jnp.zeros((16, 128), F32)
+
+    def placed(block, c):
+        total = jnp.sum(cols[c], axis=1, keepdims=True)
+        return jnp.where((lane == c) & (has_next if c == 13 else has_low), total, block)
+
+    for c in range(12):
+        block = placed(block, c)
     when_tile(-1, send_near.wait_recv)
     moment(0, wst, wgrad, HALF_SLAB, low_rows, lambda z, r, xs: nrx[z, pl.ds(r, 8), xs])
-    when_tile(1, send_window.wait_recv)
+    for send_window in send_windows:
+        when_tile(1, send_window.wait_recv)
     for z in range(depth):
         wrx[z, PAD - 1 : PAD, :] = 2.0 * wrx[z, PAD : PAD + 1, :] - wrx[z, PAD + 1 : PAD + 2, :]
     depth_gradients_of(wrx, wrx_grad, HALF_SLAB)
     gradients_of(wrx, wrx_grad, 0, HALF_SLAB)
     moment(1, wrx, wrx_grad, 0, own_rows, lambda z, r, xs: vp[z, pl.ds(PAD + height - SLAB + r, 8), xs])
 
-    row = iota((16, 128), 0)
-    lane = iota((16, 128), 1)
-    tile_index = row * 0 + t
-    has_low, has_next = tile_index > 0, tile_index < tiles - 1
-    block = jnp.zeros((16, 128), F32)
-    for c in range(14):
-        total = jnp.sum(cols[c], axis=1, keepdims=True)
-        block = jnp.where((lane == c) & (has_next if c == 13 else has_low), total, block)
+    block = placed(block, 12)
+    block = placed(block, 13)
     buf1[v] = block
     buf1[v, 13:14, :] = jnp.full((1, 128), gain[0, 0], F32)
     shares = [
@@ -469,10 +478,6 @@
     lax.fori_loop(0, RAW_CHUNKS, relay_both, 0)
     lax.fori_loop(RAW_CHUNKS, chunks, relay, 0)
 
-    def write_out(part, c):
-        rows = pl.ds(pl.multiple_of(part * half + c * CHUNK, CHUNK), CHUNK)
-        return pltpu.make_async_copy(obuf.at[rows], out.at[0, 0, rows], osem.at[part, c])
-
     def finish(c, _):
         c_row = pl.multiple_of(c * CHUNK, CHUNK)
         for part, streams in ((0, (3, 4)), (1, (2, 5))):
@@ -480,10 +485,9 @@
                 hop(stream, c).wait_recv()
 
             def put(d, value, part=part):
-                obuf[pl.ds(pl.multiple_of(part * half + d, 8), 8), :] = value
+                out[0, 0, pl.ds(pl.multiple_of(part * half + d, 8), 8), :] = value
 
             numerator_rows(v, part * half + c_row, put, c_row, streams, inverse)
-            write_out(part, c).start()
         return 0
 
     lax.fori_loop(0, chunks, finish, 0)
@@ -491,8 +495,6 @@
     def drain(c, _):
         for stream in range(2, 6):
             hop(stream, c).wait_send()
-        for part in range(2):
-            write_out(part, c).wait()
         return 0
 
     def drain_far(c, _):
@@ -504,7 +506,8 @@
     lax.fori_loop(RAW_CHUNKS, chunks, drain_far, 0)
     when_tile(1, send_margin.wait_send)
     when_tile(1, send_near.wait_send)
-    when_tile(-1, send_window.wait_send)
+    for send_window in send_windows:
+        when_tile(-1, send_window.wait_send)
     for k, passed in zip(tile_steps, passes):
         when_tile(k, passed.wait_send)
     for copy in shares + raws:
@@ -517,13 +520,12 @@
     chunks = half // CHUNK
     smem = pl.BlockSpec(memory_space=pltpu.SMEM)
     vmem = pl.BlockSpec(memory_space=pltpu.VMEM)
-    anywhere = pl.BlockSpec(memory_space=pl.ANY)
     dma = pltpu.SemaphoreType.DMA
     return pl.pallas_call(
         functools.partial(kernel, tiles, views),
         out_shape=(jax.ShapeDtypeStruct((1, 1, height, width), F32), jax.ShapeDtypeStruct((1, 12), F32)),
         in_specs=[pl.BlockSpec(memory_space=pltpu.HBM), pl.BlockSpec(memory_space=pltpu.HBM), smem, smem, smem],
-        out_specs=(anywhere, vmem),
+        out_specs=(vmem, vmem),
         scratch_shapes=[
             pltpu.VMEM((depth, height + 2 * PAD, width), F32),
             pltpu.VMEM((3, depth, height, width), F32),
@@ -544,13 +546,12 @@
             pltpu.VMEM((depth, 4, 8, width), F32),
             pltpu.VMEM((6, half, width), F32),
             pltpu.VMEM((6, half, width), F32),
-            pltpu.VMEM((height, width), F32),
             pltpu.VMEM((2, RAW_CHUNKS * CHUNK + 2 * PAD, width), F32),
             pltpu.VMEM((2, RAW_CHUNKS * CHUNK, width), F32),
             pltpu.VMEM((2, 8, width), F32),
-            dma((depth + 1,)), dma((2,)), dma((2,)), dma((2,)),
+            dma((depth + 1,)), dma((2,)), dma((2, depth)), dma((2,)),
             dma((views - 1,)), dma((views - 1,)), dma((4,)), dma((4,)),
-            dma((6, chunks)), dma((6, chunks)), dma((2, chunks)), dma((2, 8)),
+            dma((6, chunks)), dma((6, chunks)), dma((2, 8)),
         ],
         compiler_params=pltpu.CompilerParams(
             collective_id=0, has_side_effects=True, vmem_limit_bytes=52 * 1024 * 1024

time: 58.5 us -> 58.2 us (level)
  no operation moved by 1% of the time
where the time goes in v4:
time: 58.2 us; the launch traced here: 58 us
  Pallas kernels  54 us (93%)
  between operations  2.58 us (4%)
  local copies, waits for them, and re-layouts  1.48 us (3%)
    pallas_call x1, Pallas kernels, on_device(): pl.pallas_call(functools.partial(kernel, tiles, views), out_shape=(jax.Sh...  54 us
    unnamed x2, local copies, waits for them, and re-layouts  1.48 us

profile of v4, /device:TPU:24, one launch (start us, length us, event | category | flops | bytes accessed | tf_op | source)
XLA Modules:
  0.0 58.0 jit_solution(294280638549724901)
XLA Ops:
  2.6 54.0 %refine_and_join.1 = (f32[1,1,512,512]{3,2,1,0:T(8,128)S(1)}, f32[1,12]{1,0:T(1,128)S(1)}) custom-call(f32[1,1,4,512,512]{4,3,2,1,0:T(8,128)} %vol.1, f32[1,12]{1,0:T(1,128)} %aff.1, s32[1]{0:T(128)S(6)} %copy.9.slab, s32[1]{0:T(128)S(6)} %copy.10.margin, f32[1,1]{1,0:T(1,128)S(6)} %copy.11.gain), custom_call_target="tpu_custom_call" | custom-call | tf_op jit(solution)/shard_map/refine_and_join/pallas_call | solution.py:524
  56.6 1.0 %copy.12 = f32[1,1,512,512]{3,2,1,0:T(8,128)} copy(f32[1,1,512,512]{3,2,1,0:T(8,128)S(1)} %get-tuple-element.4) | data formatting | bytes 2097152
  57.5 0.5 copy.13

commit v5 on v4

--- a/solution.py
+++ b/solution.py
@@ -10,8 +10,9 @@
 MESH = pl.DeviceIdType.MESH
 F32 = jnp.float32
 SLAB = 64
-HALF_SLAB = 32
-SENT_ROWS = 40
+FIRST_ROWS = 16
+REST_ROWS = SLAB - FIRST_ROWS
+SENT_ROWS = FIRST_ROWS + 8
 STIFFNESS_FACTOR = 0.25
 PAD = 8
 CHUNK = 32
@@ -110,7 +111,7 @@
     send_margin = remote(mown, mlow, msem.at[0], msem.at[1], dev(tile_at(1), v))
     when_tile(1, send_margin.start)
     send_near = remote(
-        vol.at[0, 0, :, pl.ds(height - HALF_SLAB, HALF_SLAB)], nrx, nsem.at[0], nsem.at[1], dev(tile_at(1), v)
+        vol.at[0, 0, :, pl.ds(height - REST_ROWS, REST_ROWS)], nrx, nsem.at[0], nsem.at[1], dev(tile_at(1), v)
     )
     when_tile(1, send_near.start)
 
@@ -238,7 +239,7 @@
             for p, q in {(4 * a + i, 4 * b + j), (4 * a + j, 4 * b + i), (4 * b + i, 4 * a + j), (4 * b + j, 4 * a + i)}:
                 cols[p, q : q + 1, :] = row
 
-    def moment(part, src, srcg, first, rows, near):
+    def moment(part, src, srcg, first, count, rows, near):
         def lane_block(xl, _):
             xs = pl.ds(pl.multiple_of(xl * 128, 128), 128)
             xv = coordinate(lane8 + xl * 128, width)
@@ -257,7 +258,7 @@
                     new += [c + term for c, term in zip(carry[3 * k : 3 * k + 3], (p1, yv * p0, p0))]
                 return tuple(new)
 
-            sums = lax.fori_loop(0, HALF_SLAB // 8, body, tuple(jnp.zeros((8, 128), F32) for _ in range(9)))
+            sums = lax.fori_loop(0, count // 8, body, tuple(jnp.zeros((8, 128), F32) for _ in range(9)))
             for k in range(3):
                 zo, yo, oo = sums[3 * k : 3 * k + 3]
                 for j, term in enumerate((zo, yo, xv * oo, oo)):
@@ -281,14 +282,14 @@
     for c in range(12):
         block = placed(block, c)
     when_tile(-1, send_near.wait_recv)
-    moment(0, wst, wgrad, HALF_SLAB, low_rows, lambda z, r, xs: nrx[z, pl.ds(r, 8), xs])
+    moment(0, wst, wgrad, FIRST_ROWS, REST_ROWS, low_rows, lambda z, r, xs: nrx[z, pl.ds(r, 8), xs])
     for send_window in send_windows:
         when_tile(1, send_window.wait_recv)
     for z in range(depth):
         wrx[z, PAD - 1 : PAD, :] = 2.0 * wrx[z, PAD : PAD + 1, :] - wrx[z, PAD + 1 : PAD + 2, :]
-    depth_gradients_of(wrx, wrx_grad, HALF_SLAB)
-    gradients_of(wrx, wrx_grad, 0, HALF_SLAB)
-    moment(1, wrx, wrx_grad, 0, own_rows, lambda z, r, xs: vp[z, pl.ds(PAD + height - SLAB + r, 8), xs])
+    depth_gradients_of(wrx, wrx_grad, FIRST_ROWS)
+    gradients_of(wrx, wrx_grad, 0, FIRST_ROWS)
+    moment(1, wrx, wrx_grad, 0, FIRST_ROWS, own_rows, lambda z, r, xs: vp[z, pl.ds(PAD + height - SLAB + r, 8), xs])
 
     block = placed(block, 12)
     block = placed(block, 13)
@@ -532,8 +533,8 @@
             pltpu.VMEM((depth, SLAB + 2 * PAD, width), F32),
             pltpu.VMEM((3, depth, SLAB, width), F32),
             pltpu.VMEM((depth, SENT_ROWS + PAD, width), F32),
-            pltpu.VMEM((3, depth, HALF_SLAB, width), F32),
-            pltpu.VMEM((depth, HALF_SLAB, width), F32),
+            pltpu.VMEM((3, depth, FIRST_ROWS, width), F32),
+            pltpu.VMEM((depth, REST_ROWS, width), F32),
             pltpu.VMEM((8, 128), jnp.int32),
             pltpu.VMEM((8, 128), jnp.int32),
             pltpu.VMEM((1, 12), F32),

time: 58.2 us -> 57.8 us (level)
  no operation moved by 1% of the time
where the time goes in v5:
time: 57.8 us; the launch traced here: 57.7 us
  Pallas kernels  53.6 us (93%)
  between operations  2.58 us (4%)
  local copies, waits for them, and re-layouts  1.48 us (3%)
    pallas_call x1, Pallas kernels, on_device(): pl.pallas_call(functools.partial(kernel, tiles, views), out_shape=(jax.Sh...  53.6 us
    unnamed x2, local copies, waits for them, and re-layouts  1.48 us

profile of v5, /device:TPU:24, one launch (start us, length us, event | category | flops | bytes accessed | tf_op | source)
XLA Modules:
  0.0 57.7 jit_solution(5735488901211577413)
XLA Ops:
  2.6 53.6 %refine_and_join.1 = (f32[1,1,512,512]{3,2,1,0:T(8,128)S(1)}, f32[1,12]{1,0:T(1,128)S(1)}) custom-call(f32[1,1,4,512,512]{4,3,2,1,0:T(8,128)} %vol.1, f32[1,12]{1,0:T(1,128)} %aff.1, s32[1]{0:T(128)S(6)} %copy.9.slab, s32[1]{0:T(128)S(6)} %copy.10.margin, f32[1,1]{1,0:T(1,128)S(6)} %copy.11.gain), custom_call_target="tpu_custom_call" | custom-call | tf_op jit(solution)/shard_map/refine_and_join/pallas_call | solution.py:525
  56.2 1.0 %copy.12 = f32[1,1,512,512]{3,2,1,0:T(8,128)} copy(f32[1,1,512,512]{3,2,1,0:T(8,128)S(1)} %get-tuple-element.4) | data formatting | bytes 2097152
  57.2 0.5 copy.13

commit v6 on v5

--- a/solution.py
+++ b/solution.py
@@ -300,6 +300,8 @@
     ]
     for share in shares:
         share.start()
+    for raw in raws[4:]:
+        raw.start()
     gradients_of(vp, grads, 0, half)
     for k, share in enumerate(shares):
         share.wait_recv()
@@ -313,8 +315,6 @@
     ]
     for k, passed in zip(tile_steps, passes):
         when_tile(k, passed.start)
-    for raw in raws[4:]:
-        raw.start()
     gradients_of(vp, grads, half, height)
     across = coordinate(iota((8, width), 1), width)
     facing = 1.0 - 2.0 * lax.rem(v, 2).astype(F32)

time: 57.8 us -> 57.1 us (0.988)
  Pallas kernels: 53.6 us -> 52.9 us
    pallas_call x1, Pallas kernels: 53.6 us -> 52.9 us  [on_device(): pl.pallas_call(functools.partial(kernel, tiles, views), out_shape=(jax.Sh...]
where the time goes in v6:
time: 57.1 us; the launch traced here: 57 us
  Pallas kernels  52.9 us (93%)
  between operations  2.58 us (5%)
  local copies, waits for them, and re-layouts  1.48 us (3%)
    pallas_call x1, Pallas kernels, on_device(): pl.pallas_call(functools.partial(kernel, tiles, views), out_shape=(jax.Sh...  52.9 us
    unnamed x2, local copies, waits for them, and re-layouts  1.48 us

profile of v6, /device:TPU:24, one launch (start us, length us, event | category | flops | bytes accessed | tf_op | source)
XLA Modules:
  0.0 57.0 jit_solution(13698410682959035965)
XLA Ops:
  2.6 52.9 %refine_and_join.1 = (f32[1,1,512,512]{3,2,1,0:T(8,128)S(1)}, f32[1,12]{1,0:T(1,128)S(1)}) custom-call(f32[1,1,4,512,512]{4,3,2,1,0:T(8,128)} %vol.1, f32[1,12]{1,0:T(1,128)} %aff.1, s32[1]{0:T(128)S(6)} %copy.9.slab, s32[1]{0:T(128)S(6)} %copy.10.margin, f32[1,1]{1,0:T(1,128)S(6)} %copy.11.gain), custom_call_target="tpu_custom_call" | custom-call | tf_op jit(solution)/shard_map/refine_and_join/pallas_call | solution.py:525
  55.5 1.0 %copy.12 = f32[1,1,512,512]{3,2,1,0:T(8,128)} copy(f32[1,1,512,512]{3,2,1,0:T(8,128)S(1)} %get-tuple-element.4) | data formatting | bytes 2097152
  56.4 0.5 copy.13

commit v7 on v6

--- a/solution.py
+++ b/solution.py
@@ -17,7 +17,7 @@
 PAD = 8
 CHUNK = 32
 RAW_CHUNKS = 5
-EARLY_ROWS = 96
+EARLY_ROWS = 80
 PAIRS = ((0, 0), (0, 1), (0, 2), (1, 1), (1, 2), (2, 2))
 MONOS = ((0, 0), (0, 1), (0, 2), (0, 3), (1, 1), (1, 2), (1, 3), (2, 2), (2, 3), (3, 3))
 

time: 57.1 us -> 57.1 us (level)
  no operation moved by 1% of the time
where the time goes in v7:
time: 57.1 us; the launch traced here: 57 us
  Pallas kernels  52.9 us (93%)
  between operations  2.58 us (5%)
  local copies, waits for them, and re-layouts  1.48 us (3%)
    pallas_call x1, Pallas kernels, on_device(): pl.pallas_call(functools.partial(kernel, tiles, views), out_shape=(jax.Sh...  52.9 us
    unnamed x2, local copies, waits for them, and re-layouts  1.48 us

profile of v7, /device:TPU:24, one launch (start us, length us, event | category | flops | bytes accessed | tf_op | source)
XLA Modules:
  0.0 57.0 jit_solution(12246727183189950567)
XLA Ops:
  2.6 52.9 %refine_and_join.1 = (f32[1,1,512,512]{3,2,1,0:T(8,128)S(1)}, f32[1,12]{1,0:T(1,128)S(1)}) custom-call(f32[1,1,4,512,512]{4,3,2,1,0:T(8,128)} %vol.1, f32[1,12]{1,0:T(1,128)} %aff.1, s32[1]{0:T(128)S(6)} %copy.9.slab, s32[1]{0:T(128)S(6)} %copy.10.margin, f32[1,1]{1,0:T(1,128)S(6)} %copy.11.gain), custom_call_target="tpu_custom_call" | custom-call | tf_op jit(solution)/shard_map/refine_and_join/pallas_call | solution.py:525
  55.5 1.0 %copy.12 = f32[1,1,512,512]{3,2,1,0:T(8,128)} copy(f32[1,1,512,512]{3,2,1,0:T(8,128)S(1)} %get-tuple-element.4) | data formatting | bytes 2097152
  56.4 0.5 copy.13

commit v8 on v7

--- a/solution.py
+++ b/solution.py
@@ -17,7 +17,7 @@
 PAD = 8
 CHUNK = 32
 RAW_CHUNKS = 5
-EARLY_ROWS = 80
+EARLY_ROWS = 72
 PAIRS = ((0, 0), (0, 1), (0, 2), (1, 1), (1, 2), (2, 2))
 MONOS = ((0, 0), (0, 1), (0, 2), (0, 3), (1, 1), (1, 2), (1, 3), (2, 2), (2, 3), (3, 3))
 

time: 57.1 us -> 57.1 us (level)
  no operation moved by 1% of the time
where the time goes in v8:
time: 57.1 us; the launch traced here: 57 us
  Pallas kernels  52.9 us (93%)
  between operations  2.58 us (5%)
  local copies, waits for them, and re-layouts  1.48 us (3%)
    pallas_call x1, Pallas kernels, on_device(): pl.pallas_call(functools.partial(kernel, tiles, views), out_shape=(jax.Sh...  52.9 us
    unnamed x2, local copies, waits for them, and re-layouts  1.48 us

profile of v8, /device:TPU:24, one launch (start us, length us, event | category | flops | bytes accessed | tf_op | source)
XLA Modules:
  0.0 57.0 jit_solution(4960731435243241037)
XLA Ops:
  2.6 52.9 %refine_and_join.1 = (f32[1,1,512,512]{3,2,1,0:T(8,128)S(1)}, f32[1,12]{1,0:T(1,128)S(1)}) custom-call(f32[1,1,4,512,512]{4,3,2,1,0:T(8,128)} %vol.1, f32[1,12]{1,0:T(1,128)} %aff.1, s32[1]{0:T(128)S(6)} %copy.9.slab, s32[1]{0:T(128)S(6)} %copy.10.margin, f32[1,1]{1,0:T(1,128)S(6)} %copy.11.gain), custom_call_target="tpu_custom_call" | custom-call | tf_op jit(solution)/shard_map/refine_and_join/pallas_call | solution.py:525
  55.5 1.0 %copy.12 = f32[1,1,512,512]{3,2,1,0:T(8,128)} copy(f32[1,1,512,512]{3,2,1,0:T(8,128)S(1)} %get-tuple-element.4) | data formatting | bytes 2097152
  56.4 0.5 copy.13
